TPU v7x, 256 devices: a whole 4x4x8 slice. The times are simulated.
256 devices in a mesh: node: 8 (over z_lo, x), sht: 32 (over y, z_hi, core).
Axes of the slice: x: 4, y: 4, z: 8 (z_hi: 4, z_lo: 2; z = z_hi * 2 + z_lo), core: 2. Of those that a mesh axis runs over, the one named last changes fastest.
Arguments:
- harmonics: bfloat16 [128, 32, 2, 2048], P('sht'), may hold values from -6 to 6
- radial: float32 [16, 2, 2048], P('node'), may hold values from -6 to 6
- node_weight: float32 [16], P('node'), may hold values from 0.3 to 3
- legendre: bfloat16 [128, 2048, 512], P('sht'), may hold values from -0.125 to 0.125
- order_table: int32 [128], replicated, may hold values from 0 to 2047, as said below
- cycle_table: int32 [512], P('sht'), may hold values from 1024 to 3072, as said below
Outputs:
- gradient: float32 [128, 32, 2, 2048], P('sht', 'node')
Inputs may be any that keep to these rules, and one draw needn't show every extreme that they name: `order_table`: distinct orders; 0 and 2047 always among them. `cycle_table`: distinct cycle numbers of the equatorial belt; 1024 and 3072 always among them.
All inputs are finite; a program needn't handle non-finite values.
Results may differ from a plain program's by a relative error of at most 0.0059.
Values may be sent and summed in bfloat16 or wider, within the bound.
No kernel may reach another device: no remote copies, remote signals or barrier semaphores. Data moves between devices by JAX's collectives and lax.ppermute only.
A program may use at most 192 MiB of HBM per device.

v0:
```python
import math

import jax
import jax.numpy as jnp
from jax import lax
from jax.sharding import PartitionSpec as P

NSIDE = 1024


def fourier_tables(order_table, pixels):
    pixel_index = jnp.arange(pixels, dtype=jnp.int32)
    product_index = order_table[:, None] * pixel_index[None, :] % pixels
    phase_angle = product_index.astype(jnp.float32) * (2.0 * math.pi / pixels)
    return (jnp.cos(phase_angle).astype(jnp.bfloat16), jnp.sin(phase_angle).astype(jnp.bfloat16))


def cycle_rotation(order_table, cycle_table, pixels):
    parity = (cycle_table - NSIDE + 1) % 2
    product_index = order_table[:, None] * (2 - parity)[None, :] % (2 * pixels)
    phase_angle = product_index.astype(jnp.float32) * (math.pi / pixels)
    return (jnp.cos(phase_angle), jnp.sin(phase_angle))


def on_device(harmonics, radial, node_weight, legendre, order_table, cycle_table):
    orders_dev, samples, _, degrees = harmonics.shape
    nodes_dev = radial.shape[0]
    orders = order_table.shape[0]
    cycle_dev = cycle_table.shape[0]
    cycles = legendre.shape[2]
    pixels = 4 * NSIDE
    weighted = (harmonics[:, None, None] * radial[None, :, :, None, None, :]).astype(jnp.bfloat16)
    weighted = weighted.reshape(orders_dev, -1, degrees)
    coefficients = jnp.einsum(
        "olk,ocl->okc", legendre, weighted, preferred_element_type=jnp.float32
    ).astype(jnp.bfloat16)
    at_cycles = lax.all_to_all(coefficients, "sht", split_axis=1, concat_axis=0, tiled=True)
    cosines, sines = fourier_tables(order_table, pixels)
    rot_cos, rot_sin = cycle_rotation(order_table, cycle_table, pixels)
    pairs = at_cycles.reshape(orders, cycle_dev, -1, 2).astype(jnp.float32)
    real_part = rot_cos[:, :, None] * pairs[..., 0] - rot_sin[:, :, None] * pairs[..., 1]
    imag_part = rot_sin[:, :, None] * pairs[..., 0] + rot_cos[:, :, None] * pairs[..., 1]
    turned = jnp.concatenate([real_part, imag_part], 0).astype(jnp.bfloat16)
    synth_table = jnp.concatenate([cosines, -sines], 0)
    fields = lax.dot_general(
        turned, synth_table, (((0,), (0,)), ((), ())), preferred_element_type=jnp.float32
    ) * orders ** (-0.5)
    fields = fields.reshape(cycle_dev, nodes_dev, 2, samples, pixels)
    alpha_field = fields[:, :, 0]
    beta_field = fields[:, :, 1]
    products = jnp.stack([beta_field * beta_field, alpha_field * beta_field], 2).astype(
        jnp.bfloat16
    )
    analysis_table = jnp.concatenate([cosines, sines], 0)
    spectra = lax.dot_general(
        products, analysis_table, (((4,), (1,)), ((), ())), preferred_element_type=jnp.float32
    ) * pixels ** (-0.5)
    cos_part = spectra[..., :orders]
    sin_part = spectra[..., orders:]
    turn_cos = jnp.transpose(rot_cos)[:, None, None, None, :]
    turn_sin = jnp.transpose(rot_sin)[:, None, None, None, :]
    g_real = turn_cos * cos_part - turn_sin * sin_part
    g_imag = -(turn_sin * cos_part + turn_cos * sin_part)
    outgoing = jnp.stack([g_real, g_imag], -1).astype(jnp.bfloat16)
    outgoing = jnp.transpose(outgoing, (4, 0, 1, 2, 3, 5)).reshape(orders, cycle_dev, -1)
    at_orders = lax.all_to_all(outgoing, "sht", split_axis=0, concat_axis=1, tiled=True)
    moments = jnp.einsum("olk,okc->olc", legendre, at_orders, preferred_element_type=jnp.float32)
    moments = moments.reshape(orders_dev, degrees, nodes_dev, 2, samples, 2)
    weight_alpha = node_weight[:, None] * radial[:, 0]
    weight_beta = 2.0 * node_weight[:, None] * radial[:, 1]
    node_partial = jnp.einsum("olnsr,nl->osrl", moments[:, :, :, 0], weight_alpha) + jnp.einsum(
        "olnsr,nl->osrl", moments[:, :, :, 1], weight_beta
    )
    node_partial = node_partial * math.sqrt(degrees / cycles)
    per_node = samples // lax.axis_size("node")
    summed = lax.psum(node_partial, "node")
    result = lax.dynamic_slice_in_dim(summed, lax.axis_index("node") * per_node, per_node, 1)
    return result


def solution(mesh):
    in_specs = (
        P("sht", None, None, None),
        P("node", None, None),
        P("node"),
        P("sht", None, None),
        P(),
        P("sht"),
    )
    out_specs = P("sht", "node", None, None)
    return jax.shard_map(
        on_device, mesh=mesh, in_specs=in_specs, out_specs=out_specs, check_vma=False
    )
```

profile of v0, /device:TPU:1, one launch (start us, length us, event | category | flops | bytes accessed | tf_op | source)
XLA Modules:
  0.0 323.3 jit_solution(1413049268691856544)
XLA Ops:
  6.5 8.8 %mul.222 = f32[4,2,2,32,2,2048]{5,4,3,2,1,0:T(2,128)} broadcast(bf16[4,32,2,2048]{3,2,1,0:T(2,128)(2,1)} %param.6), dimensions={0,3,4,5} | broadcast | bytes 9437184 | tf_op jit(solution)/shard_map/mul | solution.py:32
  15.3 10.9 %mul.223 = f32[4,256,2048]{2,1,0:T(8,128)} reshape(f32[4,2,2,32,2,2048]{5,4,3,2,1,0:T(2,128)} %mul.222) | data formatting | bytes 16777216 | tf_op jit(solution)/shard_map/mul | solution.py:32
  26.2 0.0 copy-done.2
  26.2 2.4 mul.224
  28.7 2.7 mul.225
  31.4 8.1 %fusion.24 = bf16[4,512,256]{1,2,0:T(8,128)(2,1)S(1)} fusion(bf16[4,2048,512]{2,1,0:T(8,128)(2,1)} %param.9, f32[4,256,2048]{2,1,0:T(8,128)} %mul.223, f32[256,2048]{1,0:T(8,128)S(1)} %mul.225), kind=kOutput, calls=%fused_computation.38 | convolution fusion | flops 2152202240 | bytes 19922944 | tf_op jit(solution)/shard_map/olk,ocl->okc/dot_general | solution.py:34
  39.5 0.0 copy-start.5
  39.5 0.0 copy-start.3
  39.5 1.4 copy.25
  40.9 12.8 %all-to-all-start = ((bf16[4,512,256]{2,0,1:T(4,128)(2,1)}), bf16[4,512,256]{2,0,1:T(4,128)(2,1)S(1)}, u32[]{:S(2)}, u32[]{:S(2)}) async-start(bf16[4,512,256]{2,0,1:T(4,128)(2,1)} %copy.25), calls=%async_computation | async-start | bytes 2097152 | tf_op jit(solution)/shard_map/all_to_all | solution.py:37
  53.7 0.0 copy-done.5
  53.7 0.0 copy-done.3
  53.7 0.1 fusion.49
  53.9 0.1 fusion.51
  54.0 9.1 %fusion.39 = bf16[128,4096]{1,0:T(8,128)(2,1)} fusion(s32[128]{0:T(128)S(1)} %copy-done.3), kind=kLoop, calls=%fused_computation.56 | loop fusion | flops 9437184 | bytes 1049088 | tf_op jit(solution)/shard_map/neg | solution.py:44
  63.1 9.6 %sine_convert_fusion = (bf16[128,4096]{1,0:T(8,128)(2,1)}, bf16[128,4096]{1,0:T(8,128)(2,1)S(1)}) fusion(s32[128]{0:T(128)S(1)} %copy-done.3), kind=kLoop, calls=%fused_computation.32 | loop fusion | flops 8388608 | bytes 2097664 | tf_op jit(solution)/shard_map/convert_element_type | solution.py:15
  72.7 9.9 %all-to-all-done = bf16[4,512,256]{2,0,1:T(4,128)(2,1)S(1)} async-done(((bf16[4,512,256]{2,0,1:T(4,128)(2,1)}), bf16[4,512,256]{2,0,1:T(4,128)(2,1)S(1)}, u32[]{:S(2)}, u32[]{:S(2)}) %all-to-all-start) | async-done | bytes 1048608 | tf_op jit(solution)/shard_map/all_to_all | solution.py:37
  82.6 0.1 copy.26
  82.7 0.3 convert_bitcast_fusion
  83.0 8.7 %copy.27 = f32[32,4,16,256]{2,3,1,0:T(8,128)} copy(f32[32,4,16,256]{3,2,0,1:T(8,128)S(1)} %convert_bitcast_fusion) | data formatting | bytes 4194304 | tf_op jit(solution)/shard_map/convert_element_type | solution.py:40
  91.7 20.8 %fusion.56 = (f32[128,16,128,1]{1,3,2,0:T(1,128)}, f32[128,16,128,1]{1,3,2,0:T(1,128)}) fusion(f32[128,16,128,2]{1,3,2,0:T(2,128)} %bitcast.85), kind=kLoop, calls=%fused_computation.90 | loop fusion | bytes 4194304 | tf_op jit(solution)/shard_map/slice | solution.py:41
  112.5 10.4 %copy.51 = f32[128,16,128,1]{0,2,1,3:T(8,128)S(1)} copy(f32[128,16,128,1]{1,3,2,0:T(1,128)} %get-tuple-element.10) | data formatting | bytes 2097152
  122.9 10.4 %copy.50 = f32[128,16,128,1]{0,2,1,3:T(8,128)S(1)} copy(f32[128,16,128,1]{1,3,2,0:T(1,128)} %get-tuple-element.9) | data formatting | bytes 2097152
  133.3 0.0 copy-start
  133.3 0.3 fusion.34
  133.6 0.9 copy-done
  134.5 13.1 %broadcast_multiply_fusion = f32[16,128,4096]{2,1,0:T(8,128)} fusion(bf16[128,4096]{1,0:T(8,128)(2,1)S(1)} %get-tuple-element.22, bf16[128,4096]{1,0:T(8,128)(2,1)S(1)} %copy-done, bf16[128,16,128]{0,2,1:T(8,128)(2,1)S(1)} %get-tuple-element.14, bf16[128,16,128]{0,2,1:T(8,128)(2,1)S(1)} %get-tuple-element.13), kind=kOutput, calls=%fused_computation.7 | convolution fusion | flops 4309647360 | bytes 36700160 | tf_op jit(solution)/shard_map/dot_general | solution.py:45
  147.6 12.2 %multiply_convert_fusion = (bf16[16,2,1,32,4096]{4,3,2,1,0:T(8,128)(2,1)S(1)}, bf16[16,2,1,32,4096]{4,3,2,1,0:T(8,128)(2,1)S(1)}) fusion(f32[16,2,2,32,4096]{4,3,2,1,0:T(8,128)} %bitcast.84), kind=kLoop, calls=%fused_computation.6 | loop fusion | flops 16777216 | bytes 50331648 | tf_op jit(solution)/shard_map/convert.7
  159.8 0.0 copy-done.1
  159.8 5.0 %fusion.25 = f32[16,2,2,32,256]{4,3,2,1,0:T(8,128)S(1)} fusion(bf16[128,4096]{1,0:T(8,128)(2,1)S(1)} %get-tuple-element.22, bf16[128,4096]{1,0:T(8,128)(2,1)S(1)} %copy-done.1, bf16[16,2,1,32,4096]{4,3,2,1,0:T(8,128)(2,1)S(1)} %get-tuple-element.8, bf16[16,2,1,32,4096]{4,3,2,1,0:T(8,128)(2,1)S(1)} %get-tuple-element.7), kind=kOutput, calls=%fused_computation.39 | convolution fusion | flops 4308074496 | bytes 20971520 | tf_op jit(solution)/shard_map/dot_general | solution.py:55
  164.8 0.3 fusion.37
  165.1 0.1 maximum_bitcast_fusion
  165.2 0.7 copy.30
  165.9 0.0 copy-start.4
  165.9 2.1 copy.31
  168.0 5.3 %all-to-all-start.1 = ((bf16[128,16,256]{2,1,0:T(8,128)(2,1)}), bf16[128,16,256]{2,1,0:T(8,128)(2,1)S(1)}, u32[]{:S(2)}, u32[]{:S(2)}) async-start(bf16[128,16,256]{2,1,0:T(8,128)(2,1)} %copy.31), calls=%async_computation.1 | async-start | bytes 2097152 | tf_op jit(solution)/shard_map/all_to_all | solution.py:66
  173.3 0.0 all-reduce.2.cloned.1.call-start
  173.4 0.0 copy-done.4
  173.5 0.1 fusion.40
  173.5 28.3 %all-to-all-done.1 = bf16[128,16,256]{2,1,0:T(8,128)(2,1)S(1)} async-done(((bf16[128,16,256]{2,1,0:T(8,128)(2,1)}), bf16[128,16,256]{2,1,0:T(8,128)(2,1)S(1)}, u32[]{:S(2)}, u32[]{:S(2)}) %all-to-all-start.1) | async-done | bytes 1048608 | tf_op jit(solution)/shard_map/all_to_all | solution.py:66
  201.8 0.1 copy.32
  201.9 9.0 %convolution_bitcast_fusion = f32[4,2048,256]{1,2,0:T(8,128)} fusion(bf16[4,512,256]{2,1,0:T(8,128)(2,1)S(1)} %bitcast.86, bf16[4,2048,512]{2,1,0:T(8,128)(2,1)} %param.9), kind=kOutput, calls=%fused_computation.9 | convolution fusion | flops 2147483648 | bytes 17825792 | tf_op jit(solution)/shard_map/olk,okc->olc/dot_general | solution.py:67
  211.0 10.6 %reshape.142 = f32[4,2048,2,2,32,2]{1,5,4,3,2,0:T(2,128)} reshape(f32[4,2048,256]{1,2,0:T(8,128)} %convolution_bitcast_fusion) | data formatting | bytes 16777216 | tf_op jit(solution)/shard_map/reshape | solution.py:68
  221.5 9.2 %fusion.7 = (f32[2048,4,32,2]{0,3,2,1:T(2,128)S(1)}, f32[2048,4,32,2]{0,3,2,1:T(2,128)S(1)}) fusion(f32[4,2048,2,2,32,2]{1,5,4,3,2,0:T(2,128)} %reshape.142, f32[2048,2]{0,1:T(2,128)S(1)} %get-tuple-element.23, f32[2048,2]{0,1:T(2,128)S(1)} %get-tuple-element.24), kind=kLoop, calls=%fused_computation.13 | loop fusion | flops 3145728 | bytes 12615680 | tf_op jit(solution)/shard_map/olnsr,nl->osrl/dot_general | solution.py:71
  230.7 3.4 %multiply_bitcast_fusion = f32[4,32,2,2048]{3,2,1,0:T(2,128)} fusion(f32[2048,4,32,2]{0,3,2,1:T(2,128)S(1)} %get-tuple-element.6, f32[2048,4,32,2]{0,3,2,1:T(2,128)S(1)} %get-tuple-element.5), kind=kLoop, calls=%fused_computation.31 | loop fusion | flops 1048576 | bytes 6291456 | tf_op jit(solution)/shard_map/mul | solution.py:74
  234.1 0.0 all-reduce.2.cloned.1.call-update
  234.1 80.6 %all-reduce.2.cloned.1.call-done = f32[4,32,2,2048]{3,2,1,0:T(2,128)} async-done(((f32[4,32,2,2048]{3,2,1,0:T(2,128)}), f32[4,32,2,2048]{3,2,1,0:T(2,128)}) %all-reduce.2.cloned.1.call-update) | async-done | bytes 2097168 | tf_op jit(solution)/shard_map/psum | solution.py:76
  314.7 1.7 constant_dynamic-slice_fusion
  (5 shorter events, 0.0 us)
Async XLA Ops:
  15.3 10.9 %copy-start.2 = (f32[2,2,2048]{2,1,0:T(2,128)S(1)}, f32[2,2,2048]{2,1,0:T(2,128)}, u32[]{:S(2)}) copy-start(f32[2,2,2048]{2,1,0:T(2,128)} %param.7) | copy-start | bytes 98308
  39.5 14.2 %copy-start.5 = (s32[16]{0:T(128)S(1)}, s32[16]{0:T(128)}, u32[]{:S(2)}) copy-start(s32[16]{0:T(128)} %param.11) | copy-start | bytes 196
  39.5 14.2 %copy-start.3 = (s32[128]{0:T(128)S(1)}, s32[128]{0:T(128)}, u32[]{:S(2)}) copy-start(s32[128]{0:T(128)} %param.10) | copy-start | bytes 1540
  40.9 41.7 %all-to-all-start = ((bf16[4,512,256]{2,0,1:T(4,128)(2,1)}), bf16[4,512,256]{2,0,1:T(4,128)(2,1)S(1)}, u32[]{:S(2)}, u32[]{:S(2)}) async-start(bf16[4,512,256]{2,0,1:T(4,128)(2,1)} %copy.25), calls=%async_computation | async-start | bytes 2097152 | tf_op jit(solution)/shard_map/all_to_all | solution.py:37
  133.3 1.2 copy-start
  147.6 12.2 %copy-start.1 = (bf16[128,4096]{1,0:T(8,128)(2,1)S(1)}, bf16[128,4096]{1,0:T(8,128)(2,1)}, u32[]{:S(2)}) copy-start(bf16[128,4096]{1,0:T(8,128)(2,1)} %get-tuple-element.21) | copy-start | bytes 3145732
  165.9 7.5 %copy-start.4 = (f32[2]{0:T(128)S(1)}, f32[2]{0:T(128)}, u32[]{:S(2)}) copy-start(f32[2]{0:T(128)} %param.8) | copy-start | bytes 28
  168.0 33.8 %all-to-all-start.1 = ((bf16[128,16,256]{2,1,0:T(8,128)(2,1)}), bf16[128,16,256]{2,1,0:T(8,128)(2,1)S(1)}, u32[]{:S(2)}, u32[]{:S(2)}) async-start(bf16[128,16,256]{2,1,0:T(8,128)(2,1)} %copy.31), calls=%async_computation.1 | async-start | bytes 2097152 | tf_op jit(solution)/shard_map/all_to_all | solution.py:66
  173.3 141.4 %all-reduce.2.cloned.1.call-start = ((), (), s32[]{:S(2)}) async-start(), calls=%async_computation.2 | async-start | bytes 4194304 | tf_op jit(solution)/shard_map/psum | solution.py:76
Sparse Core Ops, SparseCore 0:
  234.2 80.4 all-reduce.1
where the time goes:
time: 327 us; the launch traced here: 323 us
  waiting for transfers between devices  119 us (36%)
  local copies, waits for them, and re-layouts  92.7 us (28%)
  other arithmetic  44.7 us (14%)
  matrix products  35.2 us (11%)
  starting transfers between devices  18.1 us (6%)
  between operations  13.6 us (4%)
    psum x1, waiting for transfers between devices, on_device(): summed = lax.psum(node_partial, 'node')  80.6 us
    all_to_all x1, waiting for transfers between devices, on_device(): lax.all_to_all(outgoing, 'sht', split_axis=0, concat_axis=1, tiled=True)  28.3 us
    mul x4, local copies, waits for them, and re-layouts, on_device(): harmonics[:, None, None] * radial[None, :, :, None, None, :]  24.8 us
    unnamed x14, local copies, waits for them, and re-layouts  21.7 us
    slice x1, local copies, waits for them, and re-layouts, on_device(): pairs[..., 0]  20.8 us
    dot_general x1, matrix products, on_device(): lax.dot_general(turned, synth_table, (((0,), (0,)), ((), ())), preferred_...  13.1 us
    all_to_all x1, starting transfers between devices, on_device(): lax.all_to_all(coefficients, 'sht', split_axis=1, concat_axis=0, tiled=True)  12.8 us
    another operation x2, other arithmetic  12.5 us
  transfers between devices with their start and end apart: 3, of which 3 were waited for; matrix products, arithmetic and copies ran while one was open for 6% of the time, Pallas kernels for 0%

commit v1 on v0

v1 whole, which is shorter than its diff:
```python
import functools
import math

import jax
import jax.numpy as jnp
from jax import lax
from jax.experimental import pallas as pl
from jax.experimental.pallas import tpu as pltpu
from jax.sharding import PartitionSpec as P

NSIDE = 1024
F32 = jnp.float32
BF16 = jnp.bfloat16
LANES = 128


def announce_kernel(weight_ref, radial_ref, out_ref):
    rows = []
    for n in range(2):
        for p in range(2):
            rows.append(radial_ref[n, p : p + 1, :] * (weight_ref[n] * (2.0 * (p + 1))))
    rows = jnp.concatenate(rows, 0)
    for i in range(out_ref.shape[0]):
        out_ref[i] = rows


def announce(node_weight, radial, groups):
    return pl.pallas_call(
        announce_kernel,
        in_specs=[pl.BlockSpec(memory_space=pltpu.SMEM), pl.BlockSpec(memory_space=pltpu.VMEM)],
        out_shape=jax.ShapeDtypeStruct((groups, 4, radial.shape[2]), F32),
        name="announce",
    )(node_weight, radial)


def exchange_blocks(arrays):
    arrays = list(arrays)
    block = lax.broadcasted_iota(jnp.int32, arrays[0].shape, 1) // 16
    for bit in (1, 2, 4):
        low = block & bit == 0
        for i in range(8):
            if i & bit:
                continue
            a, b = arrays[i], arrays[i | bit]
            arrays[i] = jnp.where(low, a, pltpu.roll(b, 16 * bit, 1))
            arrays[i | bit] = jnp.where(low, pltpu.roll(a, LANES - 16 * bit, 1), b)
    return arrays


def forward_kernel(harm_ref, radial_ref, leg_ref, out_ref, lines, staged):
    order = pl.program_id(0)
    samples, degrees = harm_ref.shape[1], harm_ref.shape[3]
    nodes = radial_ref.shape[0]
    groups = samples // 4
    chunks = degrees // LANES
    held = harm_ref[0].astype(F32).reshape(samples * 2, degrees)
    for lane in range(chunks):
        lines[lane] = held[:, lane * LANES : (lane + 1) * LANES]
    weighted = []
    for part in range(2):
        own = jnp.concatenate(
            [
                jnp.concatenate(
                    [
                        lines[lane, pl.ds(s * 2 + part, groups, stride=8), :]
                        for lane in range(chunks)
                    ],
                    1,
                )
                for s in range(4)
            ],
            0,
        )
        for f in range(2):
            for n in range(nodes):
                weighted.append((own * radial_ref[n, f : f + 1, :]).astype(BF16))
    coefficients = jnp.dot(
        jnp.concatenate(weighted, 0), leg_ref[0], preferred_element_type=F32
    )
    rows = nodes * samples
    for o in range(4):

        @pl.when(order == o)
        def _():
            for part in range(2):
                for f in range(2):
                    at = (part * 2 + f) * rows
                    for lane in range(staged.shape[0]):
                        staged[lane, pl.ds(f * 8 + part * 4 + o, rows, stride=16), :] = (
                            coefficients[at : at + rows, lane * LANES : (lane + 1) * LANES]
                        )

    @pl.when(order == 3)
    def _():
        size = groups * 16
        for lane in range(staged.shape[0]):
            blocks = exchange_blocks([staged[lane, i * size : (i + 1) * size, :] for i in range(8)])
            for i in range(8):
                out_ref[lane * 8 + i] = blocks[i].astype(BF16).reshape(groups, 16, LANES)


def forward(harmonics, radial, legendre):
    orders_dev, samples, _, degrees = harmonics.shape
    nodes = radial.shape[0]
    cycles = legendre.shape[2]
    out = (cycles // LANES * nodes * 4, samples // 4, 16, LANES)
    return pl.pallas_call(
        forward_kernel,
        grid=(orders_dev,),
        in_specs=[
            pl.BlockSpec((1, samples, 2, degrees), lambda o: (o, 0, 0, 0)),
            pl.BlockSpec(radial.shape, lambda o: (0, 0, 0)),
            pl.BlockSpec((1, degrees, cycles), lambda o: (o, 0, 0)),
        ],
        out_specs=pl.BlockSpec(out, lambda o: (0, 0, 0, 0)),
        scratch_shapes=[
            pltpu.VMEM((degrees // LANES, samples * 2, LANES), F32),
            pltpu.VMEM((cycles // LANES, nodes * samples * 16, LANES), F32),
        ],
        out_shape=jax.ShapeDtypeStruct(out, BF16),
        compiler_params=pltpu.CompilerParams(vmem_limit_bytes=58 * 2**20),
        cost_estimate=pl.CostEstimate(
            flops=2 * orders_dev * 256 * degrees * cycles,
            bytes_accessed=legendre.size * 2 + 2**21,
            transcendentals=0,
        ),
        name="forward",
    )(harmonics, radial, legendre)


def table_kernel(ca_ref, sa_ref, cb_ref, sb_ref, cat_ref, sat_ref, cbt_ref, sbt_ref, out_ref, flip_ref):
    high = ca_ref.shape[0]
    low = cb_ref.shape[0]
    for a in range(high):
        out_ref[a * low : (a + 1) * low, :] = (
            ca_ref[a : a + 1, :] * cb_ref[...] - sa_ref[a : a + 1, :] * sb_ref[...]
        ).astype(BF16)
    wide = cbt_ref.shape[1]
    for a in range(cat_ref.shape[1]):
        flip_ref[:, a * wide : (a + 1) * wide] = (
            cat_ref[:, a : a + 1] * cbt_ref[...] - sat_ref[:, a : a + 1] * sbt_ref[...]
        ).astype(BF16)


def angle(index, period):
    phase = (index % period).astype(F32) * (2.0 * math.pi / period)
    return jnp.cos(phase), jnp.sin(phase)


def table_orders(order_table):
    grouped = order_table.reshape(-1, 1, 4)
    rows = jnp.broadcast_to(grouped, (grouped.shape[0], 2, 4)).reshape(-1)
    quarter = jnp.broadcast_to(
        jnp.arange(2, dtype=jnp.int32)[None, :, None], (grouped.shape[0], 2, 4)
    ).reshape(-1)
    return rows, quarter


def tables(order_table, pixels):
    rows, quarter = table_orders(order_table)
    low, wide = 64, 128
    shift = quarter * (pixels // 4)
    ca, sa = angle(jnp.arange(pixels // low, dtype=jnp.int32)[:, None] * low * rows[None], pixels)
    cb, sb = angle(jnp.arange(low, dtype=jnp.int32)[:, None] * rows[None] + shift[None], pixels)
    cat, sat = angle(rows[:, None] * (jnp.arange(pixels // wide, dtype=jnp.int32) * wide)[None], pixels)
    cbt, sbt = angle(
        rows[:, None] * jnp.arange(wide, dtype=jnp.int32)[None] + shift[:, None], pixels
    )
    count = rows.shape[0]
    return pl.pallas_call(
        table_kernel,
        out_shape=[
            jax.ShapeDtypeStruct((pixels, count), BF16),
            jax.ShapeDtypeStruct((count, pixels), BF16),
        ],
        compiler_params=pltpu.CompilerParams(vmem_limit_bytes=24 * 2**20),
        cost_estimate=pl.CostEstimate(
            flops=6 * pixels * count, bytes_accessed=4 * pixels * count, transcendentals=0
        ),
        name="tables",
    )(ca, sa, cb, sb, cat, sat, cbt, sbt)


def rotation(order_table, pixels):
    rows, quarter = table_orders(order_table)
    sign = (2 * quarter - 1).astype(F32)
    columns = []
    for parity in range(2):
        cosine, sine = angle(rows * (2 - parity), 2 * pixels)
        columns += [cosine, sign * sine]
    return jnp.stack(columns, 1)


def cell_kernel(in_ref, synth_ref, analysis_ref, turn_ref, parity_ref, out_ref, products, table, sem, *, block):
    count, pixels = analysis_ref.shape
    fetch = pltpu.make_async_copy(analysis_ref, table, sem)
    fetch.start()
    groups = in_ref.shape[1]
    step = products.shape[1] // (2 * LANES)
    width = step * LANES
    odd = jnp.broadcast_to(parity_ref[...], (count, LANES)) > 0.5
    turn = [jnp.broadcast_to(turn_ref[:, i : i + 1], (count, LANES)) for i in range(4)]
    rot_cos = jnp.where(odd, turn[2], turn[0])
    rot_sin = jnp.where(odd, turn[3], turn[1])
    scale = 1.0 / (128.0 * 64.0)
    back_cos = rot_cos * scale
    back_sin = rot_sin * scale

    def swap(x):
        grouped = x.reshape(count // 8, 8, LANES)
        return jnp.concatenate([grouped[:, 4:], grouped[:, :4]], 1).reshape(count, LANES)

    for first in range(0, groups, step):
        turned = [[], []]
        for g in range(first, first + step):
            arrived = in_ref[:, g].astype(F32)
            for f in range(2):
                x = arrived[:, f * 8 : (f + 1) * 8, :].reshape(count, LANES)
                turned[f].append((rot_cos * x + rot_sin * swap(x)).astype(BF16))
        turned = jnp.concatenate(turned[0] + turned[1], 1)
        for j in range(0, pixels, block):
            fields = jnp.dot(synth_ref[j : j + block, :], turned, preferred_element_type=F32)
            alpha, beta = fields[:, :width], fields[:, width:]
            products[j : j + block, :width] = (beta * beta).astype(BF16)
            products[j : j + block, width:] = (alpha * beta).astype(BF16)
        if first == 0:
            fetch.wait()
        spectra = jnp.dot(table[...], products[...], preferred_element_type=F32)
        for g in range(step):
            parts = []
            for p in range(2):
                at = p * width + g * LANES
                x = spectra[:, at : at + LANES]
                parts.append((back_cos * x - back_sin * swap(x)).reshape(count // 8, 8, LANES))
            out_ref[first + g] = jnp.concatenate(parts, 1).astype(BF16)


def cells(arrived, synth, analysis, turn, parity, step=4, block=512):
    owners, groups, rows, lanes = arrived.shape
    pixels, count = synth.shape
    whole = pl.BlockSpec(memory_space=pltpu.VMEM)
    return pl.pallas_call(
        functools.partial(cell_kernel, block=block),
        in_specs=[whole, whole, pl.BlockSpec(memory_space=pl.ANY), whole, whole],
        out_specs=whole,
        out_shape=jax.ShapeDtypeStruct((groups, owners, rows, lanes), BF16),
        scratch_shapes=[
            pltpu.VMEM((pixels, 2 * step * lanes), BF16),
            pltpu.VMEM((count, pixels), BF16),
            pltpu.SemaphoreType.DMA,
        ],
        compiler_params=pltpu.CompilerParams(vmem_limit_bytes=36 * 2**20),
        cost_estimate=pl.CostEstimate(
            flops=2 * 2 * pixels * count * groups * 2 * lanes,
            bytes_accessed=4 * pixels * count + 2**22,
            transcendentals=0,
        ),
        name="cells",
    )(arrived, synth, analysis, turn, parity)


def backward_kernel(in_ref, known_ref, leg_ref, out_ref, staged, profile):
    order = pl.program_id(0)
    degrees = leg_ref.shape[1]
    sources, cells_in = in_ref.shape[:2]
    chunks = staged.shape[0]
    per = cells_in // chunks
    rows = sources * per

    @pl.when(order == 0)
    def _():
        for lane in range(chunks):
            blocks = exchange_blocks(
                [
                    in_ref[:, lane * per + i].astype(F32).reshape(sources * 16, LANES)
                    for i in range(per)
                ]
            )
            for i in range(per):
                for group in range(sources):
                    staged[lane, pl.ds((group * per + i) * 16, 16), :] = blocks[i][
                        group * 16 : (group + 1) * 16
                    ]
        first = lax.broadcasted_iota(jnp.int32, (8, degrees), 0) < 4
        for group in range(sources):
            for p in range(2):
                lines = [
                    jnp.broadcast_to(known_ref[group, n * 2 + p : n * 2 + p + 1, :], (8, degrees))
                    for n in range(2)
                ]
                profile[p, group] = jnp.where(first, lines[0], lines[1])

    def picked(o):
        return jnp.concatenate(
            [
                jnp.concatenate(
                    [
                        staged[lane, pl.ds(p * 8 + part * 4 + o, rows, stride=16), :].astype(BF16)
                        for lane in range(chunks)
                    ],
                    1,
                )
                for part in range(2)
                for p in range(2)
            ],
            0,
        )

    taken = lax.switch(order, [functools.partial(picked, o) for o in range(4)])
    moments = lax.dot_general(
        taken, leg_ref[0], (((1,), (1,)), ((), ())), preferred_element_type=F32
    )
    moments = moments.reshape(2, 2, sources, 8, degrees)
    for part in range(2):
        total = jnp.sum(moments[part] * profile[...], (0, 1))
        out_ref[0, :, part, :] = total[:4] + total[4:]


def backward(at_orders, known, legendre):
    sources = at_orders.shape[0]
    orders_dev, degrees, cycles = legendre.shape
    return pl.pallas_call(
        backward_kernel,
        grid=(orders_dev,),
        in_specs=[
            pl.BlockSpec(at_orders.shape, lambda o: (0, 0, 0, 0)),
            pl.BlockSpec((sources, 4, degrees), lambda o: (0, 0, 0)),
            pl.BlockSpec((1, degrees, cycles), lambda o: (o, 0, 0)),
        ],
        out_specs=pl.BlockSpec((1, 4, 2, degrees), lambda o: (o, 0, 0, 0)),
        scratch_shapes=[
            pltpu.VMEM((cycles // LANES, sources * 8 * 16, LANES), F32),
            pltpu.VMEM((2, sources, 8, degrees), F32),
        ],
        out_shape=jax.ShapeDtypeStruct((orders_dev, 4, 2, degrees), F32),
        compiler_params=pltpu.CompilerParams(vmem_limit_bytes=44 * 2**20),
        cost_estimate=pl.CostEstimate(
            flops=2 * orders_dev * 256 * degrees * cycles,
            bytes_accessed=legendre.size * 2 + 2**21,
            transcendentals=0,
        ),
        name="backward",
    )(at_orders, known, legendre)


def on_device(harmonics, radial, node_weight, legendre, order_table, cycle_table):
    pixels = 4 * NSIDE
    groups = lax.axis_size("node")
    owners = lax.axis_size("sht")
    mine = announce(node_weight, radial, groups)
    harmonics, mine = lax.optimization_barrier((harmonics, mine))
    known = lax.all_to_all(mine, "node", 0, 0, tiled=True)
    outgoing = forward(harmonics, radial, legendre)
    outgoing, known = lax.optimization_barrier((outgoing, known))
    arrived = lax.all_to_all(outgoing, "sht", 0, 0, tiled=True)
    parity = jnp.tile(((cycle_table - NSIDE + 1) % 2).astype(F32), 8)[None]
    turn = rotation(order_table, pixels)
    synth, analysis = tables(order_table, pixels)
    returning = cells(arrived, synth, analysis, turn, parity)
    returning = returning.reshape(groups * owners, 16, LANES)
    at_orders = lax.all_to_all(returning, ("node", "sht"), 0, 0, tiled=True)
    at_orders = at_orders.reshape(groups, owners, 16, LANES)
    return backward(at_orders, known, legendre)


def solution(mesh):
    in_specs = (
        P("sht", None, None, None),
        P("node", None, None),
        P("node"),
        P("sht", None, None),
        P(),
        P("sht"),
    )
    out_specs = P("sht", "node", None, None)
    return jax.shard_map(
        on_device, mesh=mesh, in_specs=in_specs, out_specs=out_specs, check_vma=False
    )
```

time: 327 us -> 119 us (0.36)
  waiting for transfers between devices: 119 us -> 17.9 us
  local copies, waits for them, and re-layouts: 92.7 us -> 7.18 us
  blocking collectives: 0 us -> 44.7 us
  other arithmetic: 44.7 us -> 1.93 us
  matrix products: 35.2 us -> 0 us
  Pallas kernels: 0 us -> 28.9 us
  between operations: 13.6 us -> 0.17 us
    psum x1 -> x0, waiting for transfers between devices: 80.6 us -> none  [on_device(): summed = lax.psum(node_partial, 'node')]
    all_to_all x0 -> x1, blocking collectives: none -> 44.7 us  [on_device(): at_orders = lax.all_to_all(returning, ('node', 'sht'), 0, 0, tiled=True)]
    dot_general x4 -> x0, matrix products: 35.2 us -> none  [the longest x1 13.1 us: on_device(): lax.dot_general(turned, synth_table, (((0,), (0,)), ((), ())), preferred_...]
    pallas_call x0 -> x5, Pallas kernels: none -> 28.9 us  [the longest x1 10.1 us: cells(): pl.pallas_call(functools.partial(cell_kernel, block=block), in_specs=[who...]
    mul x4 -> x2, local copies, waits for them, and re-layouts: 24.8 us -> 0.23 us  [the longest x1 0.11 us: tables(): shift = quarter * (pixels // 4)]
    slice x2 -> x0, local copies, waits for them, and re-layouts: 20.9 us -> none  [the longest x1 20.8 us: on_device(): pairs[..., 0]]
    all_to_all x2, waiting for transfers between devices: 38.2 us -> 17.9 us  [the longest x1 17.9 us: on_device(): arrived = lax.all_to_all(outgoing, 'sht', 0, 0, tiled=True)]
    unnamed x14 -> x10, local copies, waits for them, and re-layouts: 21.7 us -> 6.31 us
  transfers between devices with their start and end apart: 3 -> 2, of which waited for: 3 -> 1; matrix products, arithmetic and copies ran while one was open for 6% -> 2% of each run, Pallas kernels for 0% -> 10%
where the time goes in v1:
time: 119 us; the launch traced here: 118 us
  blocking collectives  44.7 us (38%)
  Pallas kernels  28.9 us (24%)
  waiting for transfers between devices  17.9 us (15%)
  starting transfers between devices  17.6 us (15%)
  local copies, waits for them, and re-layouts  7.18 us (6%)
  other arithmetic  1.93 us (2%)
    all_to_all x1, blocking collectives, on_device(): at_orders = lax.all_to_all(returning, ('node', 'sht'), 0, 0, tiled=True)  44.7 us
    all_to_all x1, waiting for transfers between devices, on_device(): arrived = lax.all_to_all(outgoing, 'sht', 0, 0, tiled=True)  17.9 us
    all_to_all x1, starting transfers between devices, on_device(): arrived = lax.all_to_all(outgoing, 'sht', 0, 0, tiled=True)  11.4 us
    pallas_call x1, Pallas kernels, cells(): pl.pallas_call(functools.partial(cell_kernel, block=block), in_specs=[who...  10.1 us
    pallas_call x1, Pallas kernels, forward(): pl.pallas_call(forward_kernel, grid=(orders_dev,), in_specs=[pl.BlockSpec...  8.52 us
    unnamed x10, local copies, waits for them, and re-layouts  6.31 us
    all_to_all x1, starting transfers between devices, on_device(): known = lax.all_to_all(mine, 'node', 0, 0, tiled=True)  6.2 us
    pallas_call x1, Pallas kernels, backward(): pl.pallas_call(backward_kernel, grid=(orders_dev,), in_specs=[pl.BlockSpe...  6.04 us
  transfers between devices with their start and end apart: 2, of which 1 were waited for; matrix products, arithmetic and copies ran while one was open for 2% of the time, Pallas kernels for 10%

profile of v1, /device:TPU:1, one launch (start us, length us, event | category | flops | bytes accessed | tf_op | source)
XLA Modules:
  0.0 118.4 jit_solution(13988325281213000329)
XLA Ops:
  0.0 1.5 %announce.1 = f32[8,4,2048]{2,1,0:T(4,128)} custom-call(f32[2]{0:T(128)} %weight_ref.1, f32[2,2,2048]{2,1,0:T(2,128)} %radial_ref.3), custom_call_target="tpu_custom_call" | custom-call | tf_op jit(solution)/shard_map/announce/pallas_call | solution.py:28
  1.5 6.2 %all-to-all-start = ((f32[8,4,2048]{2,1,0:T(4,128)}), f32[8,4,2048]{2,1,0:T(4,128)S(1)}, u32[]{:S(2)}, u32[]{:S(2)}) async-start(f32[8,4,2048]{2,1,0:T(4,128)} %announce.1), calls=%async_computation | async-start | bytes 524288 | tf_op jit(solution)/shard_map/all_to_all | solution.py:352
  7.7 0.0 copy-start.4
  7.7 8.5 %forward.1 = bf16[32,8,16,128]{3,2,1,0:T(8,128)(2,1)} custom-call(bf16[4,32,2,2048]{3,2,1,0:T(2,128)(2,1)} %harm_ref, f32[2,2,2048]{2,1,0:T(2,128)} %radial_ref.3, bf16[4,2048,512]{2,1,0:T(8,128)(2,1)} %leg_ref.3), custom_call_target="tpu_custom_call" | custom-call | flops 2147483648 | bytes 10485760 | tf_op jit(solution)/shard_map/forward/pallas_call | solution.py:107
  16.2 0.0 copy-start.3
  16.2 0.0 all-to-all-done.known_ref
  16.2 11.4 %all-to-all-start.1 = ((bf16[32,8,16,128]{3,2,1,0:T(8,128)(2,1)}), bf16[32,8,16,128]{3,2,1,0:T(8,128)(2,1)S(1)}, u32[]{:S(2)}, u32[]{:S(2)}) async-start(bf16[32,8,16,128]{3,2,1,0:T(8,128)(2,1)} %forward.1), calls=%async_computation.1 | async-start | bytes 2097152 | tf_op jit(solution)/shard_map/all_to_all | solution.py:355
  27.7 0.0 copy-done.4
  27.7 0.0 copy-done.3
  27.7 0.1 broadcast_in_dim.12
  27.8 0.1 mul.194
  28.0 0.1 reshape.202
  28.1 0.1 broadcast_in_dim_tile.3.parity_ref
  28.2 0.1 mul.202
  28.3 0.1 convert_element_type.70
  28.4 0.1 fusion.13
  28.5 0.1 copy.14
  28.6 0.1 fusion.25
  28.7 0.1 sine_multiply_fusion.1
  28.8 0.1 copy.15.turn_ref
  29.0 0.6 fusion.3
  29.6 0.5 fusion.11
  30.1 0.5 multiply_sine_fusion
  30.6 2.7 %tables.1 = (bf16[4096,256]{1,0:T(8,128)(2,1)S(1)}, bf16[256,4096]{1,0:T(8,128)(2,1)S(1)}) custom-call(f32[64,256]{1,0:T(8,128)S(1)} %get-tuple-element.33.ca_ref, f32[64,256]{1,0:T(8,128)S(1)} %get-tuple-element.34.sa_ref, f32[64,256]{1,0:T(8,128)S(1)} %get-tuple-element.26.cb_ref, f32[64,256]{1,0:T(8,128)S(1)} %get-tuple-element.25.sb_ref, ...), custom_call_target="tpu_custom_call" | custom-call | flops 6291456 | bytes 4194304 | tf_op jit(solution)/shard_map/tables/pallas_call | solution.py:170
  33.4 0.0 copy-start.1
  33.4 1.3 %copy-done.1 = bf16[256,4096]{1,0:T(8,128)(2,1)} copy-done((bf16[256,4096]{1,0:T(8,128)(2,1)}, bf16[256,4096]{1,0:T(8,128)(2,1)S(1)}, u32[]{:S(2)}) %copy-start.1) | copy-done | bytes 2097176
  34.7 17.9 %all-to-all-done.1.in_ref = bf16[32,8,16,128]{3,2,1,0:T(8,128)(2,1)S(1)} async-done(((bf16[32,8,16,128]{3,2,1,0:T(8,128)(2,1)}), bf16[32,8,16,128]{3,2,1,0:T(8,128)(2,1)S(1)}, u32[]{:S(2)}, u32[]{:S(2)}) %all-to-all-start.1) | async-done | bytes 1048608 | tf_op jit(solution)/shard_map/all_to_all | solution.py:355
  52.6 0.0 copy-start.2
  52.6 1.6 %copy-done.2 = bf16[256,4096]{1,0:T(8,128)(2,1)S(1)} copy-done((bf16[256,4096]{1,0:T(8,128)(2,1)S(1)}, bf16[256,4096]{1,0:T(8,128)(2,1)}, u32[]{:S(2)}) %copy-start.2) | copy-done | bytes 2097176
  54.2 10.1 %cells.1 = bf16[8,32,16,128]{3,2,1,0:T(8,128)(2,1)S(1)} custom-call(bf16[32,8,16,128]{3,2,1,0:T(8,128)(2,1)S(1)} %all-to-all-done.1.in_ref, bf16[4096,256]{1,0:T(8,128)(2,1)S(1)} %get-tuple-element.14.synth_ref, bf16[256,4096]{1,0:T(8,128)(2,1)S(1)} %copy-done.2, f32[256,4]{1,0:T(8,128)S(1)} %copy.15.turn_ref, f32[1,128]{1,0:T(1,128)S(1)} %broadcast_in_dim_tile.3.parity_ref), custom_call_target="tpu_custom_call" | custom-call | flops 8589934592 | bytes 8388608 | tf_op jit(solution)/shard_map/cells/pallas_call | solution.py:242
  64.3 44.7 %all_to_all.15 = bf16[256,16,128]{2,1,0:T(8,128)(2,1)S(1)} all-to-all(bf16[256,16,128]{2,1,0:T(8,128)(2,1)S(1)} %bitcast.3), channel_id=1, replica_groups=mesh['node'=8,'sht'=32] {'node','sht'}, dimensions={0} | all-to-all | bytes 2097152 | tf_op jit(solution)/shard_map/all_to_all | solution.py:361
  109.0 0.0 copy-start
  109.0 3.4 %copy-done = bf16[4,2048,512]{2,1,0:T(8,128)(2,1)S(1)} copy-done((bf16[4,2048,512]{2,1,0:T(8,128)(2,1)S(1)}, bf16[4,2048,512]{2,1,0:T(8,128)(2,1)}, u32[]{:S(2)}) %copy-start) | copy-done | bytes 8388632
  112.3 6.0 %backward.1 = f32[4,4,2,2048]{3,2,1,0:T(2,128)} custom-call(bf16[8,32,16,128]{3,2,1,0:T(8,128)(2,1)S(1)} %bitcast.2, f32[8,4,2048]{2,1,0:T(4,128)S(1)} %all-to-all-done.known_ref, bf16[4,2048,512]{2,1,0:T(8,128)(2,1)S(1)} %copy-done), custom_call_target="tpu_custom_call" | custom-call | flops 2147483648 | bytes 10485760 | tf_op jit(solution)/shard_map/backward/pallas_call | solution.py:322
  (8 shorter events, 0.1 us)
Async XLA Ops:
  1.5 14.7 %all-to-all-start = ((f32[8,4,2048]{2,1,0:T(4,128)}), f32[8,4,2048]{2,1,0:T(4,128)S(1)}, u32[]{:S(2)}, u32[]{:S(2)}) async-start(f32[8,4,2048]{2,1,0:T(4,128)} %announce.1), calls=%async_computation | async-start | bytes 524288 | tf_op jit(solution)/shard_map/all_to_all | solution.py:352
  7.7 20.0 %copy-start.4 = (s32[16]{0:T(128)S(1)}, s32[16]{0:T(128)}, u32[]{:S(2)}) copy-start(s32[16]{0:T(128)} %param.11) | copy-start | bytes 196
  16.2 11.5 %copy-start.3 = (s32[128]{0:T(128)S(1)}, s32[128]{0:T(128)}, u32[]{:S(2)}) copy-start(s32[128]{0:T(128)} %param.10) | copy-start | bytes 1540
  16.2 36.3 %all-to-all-start.1 = ((bf16[32,8,16,128]{3,2,1,0:T(8,128)(2,1)}), bf16[32,8,16,128]{3,2,1,0:T(8,128)(2,1)S(1)}, u32[]{:S(2)}, u32[]{:S(2)}) async-start(bf16[32,8,16,128]{3,2,1,0:T(8,128)(2,1)} %forward.1), calls=%async_computation.1 | async-start | bytes 2097152 | tf_op jit(solution)/shard_map/all_to_all | solution.py:355
  33.4 1.3 %copy-start.1 = (bf16[256,4096]{1,0:T(8,128)(2,1)}, bf16[256,4096]{1,0:T(8,128)(2,1)S(1)}, u32[]{:S(2)}) copy-start(bf16[256,4096]{1,0:T(8,128)(2,1)S(1)} %get-tuple-element.15.analysis_ref) | copy-start | bytes 6291460
  52.6 1.6 %copy-start.2 = (bf16[256,4096]{1,0:T(8,128)(2,1)S(1)}, bf16[256,4096]{1,0:T(8,128)(2,1)}, u32[]{:S(2)}) copy-start(bf16[256,4096]{1,0:T(8,128)(2,1)} %copy-done.1) | copy-start | bytes 6291460
  109.0 3.4 %copy-start = (bf16[4,2048,512]{2,1,0:T(8,128)(2,1)S(1)}, bf16[4,2048,512]{2,1,0:T(8,128)(2,1)}, u32[]{:S(2)}) copy-start(bf16[4,2048,512]{2,1,0:T(8,128)(2,1)} %leg_ref.3) | copy-start | bytes 25165828

commit v2 on v1

--- a/solution.py
+++ b/solution.py
@@ -12,25 +12,6 @@
 F32 = jnp.float32
 BF16 = jnp.bfloat16
 LANES = 128
-
-
-def announce_kernel(weight_ref, radial_ref, out_ref):
-    rows = []
-    for n in range(2):
-        for p in range(2):
-            rows.append(radial_ref[n, p : p + 1, :] * (weight_ref[n] * (2.0 * (p + 1))))
-    rows = jnp.concatenate(rows, 0)
-    for i in range(out_ref.shape[0]):
-        out_ref[i] = rows
-
-
-def announce(node_weight, radial, groups):
-    return pl.pallas_call(
-        announce_kernel,
-        in_specs=[pl.BlockSpec(memory_space=pltpu.SMEM), pl.BlockSpec(memory_space=pltpu.VMEM)],
-        out_shape=jax.ShapeDtypeStruct((groups, 4, radial.shape[2]), F32),
-        name="announce",
-    )(node_weight, radial)
 
 
 def exchange_blocks(arrays):
@@ -191,10 +172,12 @@
     return jnp.stack(columns, 1)
 
 
-def cell_kernel(in_ref, synth_ref, analysis_ref, turn_ref, parity_ref, out_ref, products, table, sem, *, block):
+def cell_kernel(in_ref, synth_ref, analysis_ref, turn_ref, parity_ref, out_ref, products, synth, analysis, sems, *, block):
     count, pixels = analysis_ref.shape
-    fetch = pltpu.make_async_copy(analysis_ref, table, sem)
-    fetch.start()
+    fetch_synth = pltpu.make_async_copy(synth_ref, synth, sems.at[0])
+    fetch_analysis = pltpu.make_async_copy(analysis_ref, analysis, sems.at[1])
+    fetch_synth.start()
+    fetch_analysis.start()
     groups = in_ref.shape[1]
     step = products.shape[1] // (2 * LANES)
     width = step * LANES
@@ -218,14 +201,16 @@
                 x = arrived[:, f * 8 : (f + 1) * 8, :].reshape(count, LANES)
                 turned[f].append((rot_cos * x + rot_sin * swap(x)).astype(BF16))
         turned = jnp.concatenate(turned[0] + turned[1], 1)
+        if first == 0:
+            fetch_synth.wait()
         for j in range(0, pixels, block):
-            fields = jnp.dot(synth_ref[j : j + block, :], turned, preferred_element_type=F32)
+            fields = jnp.dot(synth[j : j + block, :], turned, preferred_element_type=F32)
             alpha, beta = fields[:, :width], fields[:, width:]
             products[j : j + block, :width] = (beta * beta).astype(BF16)
             products[j : j + block, width:] = (alpha * beta).astype(BF16)
         if first == 0:
-            fetch.wait()
-        spectra = jnp.dot(table[...], products[...], preferred_element_type=F32)
+            fetch_analysis.wait()
+        spectra = jnp.dot(analysis[...], products[...], preferred_element_type=F32)
         for g in range(step):
             parts = []
             for p in range(2):
@@ -239,17 +224,19 @@
     owners, groups, rows, lanes = arrived.shape
     pixels, count = synth.shape
     whole = pl.BlockSpec(memory_space=pltpu.VMEM)
+    anywhere = pl.BlockSpec(memory_space=pltpu.HBM)
     return pl.pallas_call(
         functools.partial(cell_kernel, block=block),
-        in_specs=[whole, whole, pl.BlockSpec(memory_space=pl.ANY), whole, whole],
+        in_specs=[whole, anywhere, anywhere, whole, whole],
         out_specs=whole,
         out_shape=jax.ShapeDtypeStruct((groups, owners, rows, lanes), BF16),
         scratch_shapes=[
             pltpu.VMEM((pixels, 2 * step * lanes), BF16),
+            pltpu.VMEM((pixels, count), BF16),
             pltpu.VMEM((count, pixels), BF16),
-            pltpu.SemaphoreType.DMA,
+            pltpu.SemaphoreType.DMA((2,)),
         ],
-        compiler_params=pltpu.CompilerParams(vmem_limit_bytes=36 * 2**20),
+        compiler_params=pltpu.CompilerParams(vmem_limit_bytes=50 * 2**20),
         cost_estimate=pl.CostEstimate(
             flops=2 * 2 * pixels * count * groups * 2 * lanes,
             bytes_accessed=4 * pixels * count + 2**22,
@@ -259,17 +246,25 @@
     )(arrived, synth, analysis, turn, parity)
 
 
-def backward_kernel(in_ref, known_ref, leg_ref, out_ref, staged, profile):
-    order = pl.program_id(0)
-    degrees = leg_ref.shape[1]
+def backward_kernel(
+    place_ref, in_ref, near_ref, far_ref, leg_ref, out_ref, staged, profile, leg, sems
+):
+    step = pl.program_id(0)
+    orders_dev, degrees = leg_ref.shape[:2]
     sources, cells_in = in_ref.shape[:2]
     chunks = staged.shape[0]
     per = cells_in // chunks
     rows = sources * per
 
-    @pl.when(order == 0)
+    def fetch(o):
+        return pltpu.make_async_copy(leg_ref.at[o], leg.at[o], sems.at[o])
+
+    @pl.when(step == 0)
     def _():
-        for lane in range(chunks):
+        for o in range(orders_dev):
+            fetch(o).start()
+
+        def chunk(lane, carry):
             blocks = exchange_blocks(
                 [
                     in_ref[:, lane * per + i].astype(F32).reshape(sources * 16, LANES)
@@ -281,17 +276,23 @@
                     staged[lane, pl.ds((group * per + i) * 16, 16), :] = blocks[i][
                         group * 16 : (group + 1) * 16
                     ]
+            return carry
+
+        lax.fori_loop(0, chunks, chunk, 0)
         first = lax.broadcasted_iota(jnp.int32, (8, degrees), 0) < 4
-        for group in range(sources):
-            for p in range(2):
-                lines = [
-                    jnp.broadcast_to(known_ref[group, n * 2 + p : n * 2 + p + 1, :], (8, degrees))
-                    for n in range(2)
-                ]
-                profile[p, group] = jnp.where(first, lines[0], lines[1])
-
-    def picked(o):
-        return jnp.concatenate(
+        for z, ref in enumerate((near_ref, far_ref)):
+            for x in range(ref.shape[0]):
+                group = (place_ref[0] ^ z) * 4 + (place_ref[1] ^ x)
+                for p in range(2):
+                    lines = [
+                        jnp.broadcast_to(ref[x, n, p : p + 1, :], (8, degrees)) for n in range(2)
+                    ]
+                    profile[p, group] = jnp.where(first, lines[0], lines[1])
+
+    @pl.when(step > 0)
+    def _():
+        o = step - 1
+        taken = jnp.concatenate(
             [
                 jnp.concatenate(
                     [
@@ -305,62 +306,80 @@
             ],
             0,
         )
-
-    taken = lax.switch(order, [functools.partial(picked, o) for o in range(4)])
-    moments = lax.dot_general(
-        taken, leg_ref[0], (((1,), (1,)), ((), ())), preferred_element_type=F32
-    )
-    moments = moments.reshape(2, 2, sources, 8, degrees)
-    for part in range(2):
-        total = jnp.sum(moments[part] * profile[...], (0, 1))
-        out_ref[0, :, part, :] = total[:4] + total[4:]
-
-
-def backward(at_orders, known, legendre):
+        fetch(o).wait()
+        moments = lax.dot_general(
+            taken, leg[o], (((1,), (1,)), ((), ())), preferred_element_type=F32
+        )
+        moments = moments.reshape(2, 2, sources, 8, degrees)
+        for part in range(2):
+            total = jnp.sum(moments[part] * profile[...], (0, 1))
+            out_ref[0, :, part, :] = total[:4] + total[4:]
+
+
+def backward(place, at_orders, profiles, legendre):
     sources = at_orders.shape[0]
     orders_dev, degrees, cycles = legendre.shape
+    near = profiles[0].shape
     return pl.pallas_call(
         backward_kernel,
-        grid=(orders_dev,),
-        in_specs=[
-            pl.BlockSpec(at_orders.shape, lambda o: (0, 0, 0, 0)),
-            pl.BlockSpec((sources, 4, degrees), lambda o: (0, 0, 0)),
-            pl.BlockSpec((1, degrees, cycles), lambda o: (o, 0, 0)),
-        ],
-        out_specs=pl.BlockSpec((1, 4, 2, degrees), lambda o: (o, 0, 0, 0)),
-        scratch_shapes=[
-            pltpu.VMEM((cycles // LANES, sources * 8 * 16, LANES), F32),
-            pltpu.VMEM((2, sources, 8, degrees), F32),
-        ],
+        grid_spec=pltpu.PrefetchScalarGridSpec(
+            num_scalar_prefetch=1,
+            grid=(orders_dev + 1,),
+            in_specs=[
+                pl.BlockSpec(at_orders.shape, lambda o, place: (0, 0, 0, 0)),
+                *[pl.BlockSpec(near, lambda o, place: (0, 0, 0, 0))] * 2,
+                pl.BlockSpec(memory_space=pltpu.HBM),
+            ],
+            out_specs=pl.BlockSpec(
+                (1, 4, 2, degrees), lambda o, place: (jnp.maximum(o - 1, 0), 0, 0, 0)
+            ),
+            scratch_shapes=[
+                pltpu.VMEM((cycles // LANES, sources * 8 * 16, LANES), F32),
+                pltpu.VMEM((2, sources, 8, degrees), F32),
+                pltpu.VMEM(legendre.shape, BF16),
+                pltpu.SemaphoreType.DMA((orders_dev,)),
+            ],
+        ),
         out_shape=jax.ShapeDtypeStruct((orders_dev, 4, 2, degrees), F32),
-        compiler_params=pltpu.CompilerParams(vmem_limit_bytes=44 * 2**20),
+        compiler_params=pltpu.CompilerParams(vmem_limit_bytes=52 * 2**20),
         cost_estimate=pl.CostEstimate(
             flops=2 * orders_dev * 256 * degrees * cycles,
             bytes_accessed=legendre.size * 2 + 2**21,
             transcendentals=0,
         ),
         name="backward",
-    )(at_orders, known, legendre)
+    )(place, at_orders, *profiles, legendre)
+
+
+def swapped(value, bit):
+    return lax.ppermute(value, "node", [(i, i ^ bit) for i in range(lax.axis_size("node"))])
 
 
 def on_device(harmonics, radial, node_weight, legendre, order_table, cycle_table):
     pixels = 4 * NSIDE
     groups = lax.axis_size("node")
     owners = lax.axis_size("sht")
-    mine = announce(node_weight, radial, groups)
-    harmonics, mine = lax.optimization_barrier((harmonics, mine))
-    known = lax.all_to_all(mine, "node", 0, 0, tiled=True)
     outgoing = forward(harmonics, radial, legendre)
-    outgoing, known = lax.optimization_barrier((outgoing, known))
+    outgoing, radial, node_weight, order_table, cycle_table = lax.optimization_barrier(
+        (outgoing, radial, node_weight, order_table, cycle_table)
+    )
     arrived = lax.all_to_all(outgoing, "sht", 0, 0, tiled=True)
     parity = jnp.tile(((cycle_table - NSIDE + 1) % 2).astype(F32), 8)[None]
     turn = rotation(order_table, pixels)
     synth, analysis = tables(order_table, pixels)
+    radial, synth = lax.optimization_barrier((radial, synth))
+    profile = radial * node_weight[:, None, None] * jnp.array([2.0, 4.0], F32)[None, :, None]
+    near = jnp.stack([profile] + [swapped(profile, bit) for bit in (1, 2, 3)])
+    arrived, near = lax.optimization_barrier((arrived, near))
+    far = swapped(near, 4)
     returning = cells(arrived, synth, analysis, turn, parity)
+    returning, far = lax.optimization_barrier((returning, far))
     returning = returning.reshape(groups * owners, 16, LANES)
     at_orders = lax.all_to_all(returning, ("node", "sht"), 0, 0, tiled=True)
     at_orders = at_orders.reshape(groups, owners, 16, LANES)
-    return backward(at_orders, known, legendre)
+    node = lax.axis_index("node").astype(jnp.int32)
+    place = jnp.stack([node // 4, node % 4])
+    return backward(place, at_orders, (near, far), legendre)
 
 
 def solution(mesh):

time: 119 us -> 111 us (0.933)
  blocking collectives: 44.7 us -> 0 us
  waiting for transfers between devices: 17.9 us -> 48.4 us
  starting transfers between devices: 17.6 us -> 25.6 us
  local copies, waits for them, and re-layouts: 7.18 us -> 3.53 us
  Pallas kernels: 28.9 us -> 30.1 us
    all_to_all x1 -> x0, blocking collectives: 44.7 us -> none  [on_device(): at_orders = lax.all_to_all(returning, ('node', 'sht'), 0, 0, tiled=True)]
    all_to_all x1, waiting for transfers between devices: 0.01 us -> 32 us  [on_device(): at_orders = lax.all_to_all(returning, ('node', 'sht'), 0, 0, tiled=True)]
    ppermute x0 -> x4, starting transfers between devices: none -> 5.17 us  [swapped(): lax.ppermute(value, 'node', [(i, i ^ bit) for i in range(lax.axis_size('n...]
    all_to_all x1, waiting for transfers between devices: 17.9 us -> 13.1 us  [on_device(): arrived = lax.all_to_all(outgoing, 'sht', 0, 0, tiled=True)]
    unnamed x10 -> x14, local copies, waits for them, and re-layouts: 6.31 us -> 2.66 us
    ppermute x0 -> x4, waiting for transfers between devices: none -> 3.3 us  [swapped(): lax.ppermute(value, 'node', [(i, i ^ bit) for i in range(lax.axis_size('n...]
    pallas_call x1, Pallas kernels: 10.1 us -> 12.1 us  [cells(): pl.pallas_call(functools.partial(cell_kernel, block=block), in_specs=[who...]
    all_to_all x1, starting transfers between devices: 11.4 us -> 12.9 us  [on_device(): arrived = lax.all_to_all(outgoing, 'sht', 0, 0, tiled=True)]
  transfers between devices with their start and end apart: 2 -> 6, of which waited for: 1 -> 4; matrix products, arithmetic and copies ran while one was open for 2% -> 3% of each run, Pallas kernels for 10% -> 13%
where the time goes in v2:
time: 111 us; the launch traced here: 110 us
  waiting for transfers between devices  48.4 us (44%)
  Pallas kernels  30.1 us (27%)
  starting transfers between devices  25.6 us (23%)
  local copies, waits for them, and re-layouts  3.53 us (3%)
  other arithmetic  2.24 us (2%)
    all_to_all x1, waiting for transfers between devices, on_device(): at_orders = lax.all_to_all(returning, ('node', 'sht'), 0, 0, tiled=True)  32 us
    all_to_all x1, waiting for transfers between devices, on_device(): arrived = lax.all_to_all(outgoing, 'sht', 0, 0, tiled=True)  13.1 us
    all_to_all x1, starting transfers between devices, on_device(): arrived = lax.all_to_all(outgoing, 'sht', 0, 0, tiled=True)  12.9 us
    pallas_call x1, Pallas kernels, cells(): pl.pallas_call(functools.partial(cell_kernel, block=block), in_specs=[who...  12.1 us
    pallas_call x1, Pallas kernels, forward(): pl.pallas_call(forward_kernel, grid=(orders_dev,), in_specs=[pl.BlockSpec...  8.52 us
    all_to_all x1, starting transfers between devices, on_device(): at_orders = lax.all_to_all(returning, ('node', 'sht'), 0, 0, tiled=True)  7.56 us
    pallas_call x1, Pallas kernels, backward(): pl.pallas_call(backward_kernel, grid_spec=pltpu.PrefetchScalarGridSpec(nu...  6.78 us
    ppermute x4, starting transfers between devices, swapped(): lax.ppermute(value, 'node', [(i, i ^ bit) for i in range(lax.axis_size('n...  5.17 us
  transfers between devices with their start and end apart: 6, of which 4 were waited for; matrix products, arithmetic and copies ran while one was open for 3% of the time, Pallas kernels for 13%

profile of v2, /device:TPU:1, one launch (start us, length us, event | category | flops | bytes accessed | tf_op | source)
XLA Modules:
  0.0 110.3 jit_solution(5224981190194945052)
XLA Ops:
  0.0 8.5 %forward.1 = bf16[32,8,16,128]{3,2,1,0:T(8,128)(2,1)} custom-call(bf16[4,32,2,2048]{3,2,1,0:T(2,128)(2,1)} %harm_ref.1, f32[2,2,2048]{2,1,0:T(2,128)} %radial_ref.1, bf16[4,2048,512]{2,1,0:T(8,128)(2,1)} %leg_ref.3), custom_call_target="tpu_custom_call" | custom-call | flops 2147483648 | bytes 10485760 | tf_op jit(solution)/shard_map/forward/pallas_call | solution.py:88
  8.5 0.0 copy-start.5
  8.5 0.0 copy-start.2
  8.5 0.0 copy-start.3
  8.5 0.0 copy-start.4
  8.5 0.0 copy-start.6
  8.6 12.9 %all-to-all-start = ((bf16[32,8,16,128]{3,2,1,0:T(8,128)(2,1)}), bf16[32,8,16,128]{3,2,1,0:T(8,128)(2,1)S(1)}, u32[]{:S(2)}, u32[]{:S(2)}) async-start(bf16[32,8,16,128]{3,2,1,0:T(8,128)(2,1)} %forward.1), calls=%async_computation | async-start | bytes 2097152 | tf_op jit(solution)/shard_map/all_to_all | solution.py:366
  21.5 0.0 copy-done.5
  21.5 0.1 broadcast_in_dim.12
  21.6 0.1 mul.210
  21.7 0.1 mul.218
  21.9 0.1 fusion.13
  22.0 0.1 copy.15
  22.0 0.5 multiply_sine_fusion
  22.5 0.5 fusion.11
  23.1 0.6 fusion.3
  23.7 2.7 %tables.1 = (bf16[4096,256]{1,0:T(8,128)(2,1)S(1)}, bf16[256,4096]{1,0:T(8,128)(2,1)S(1)}) custom-call(f32[64,256]{1,0:T(8,128)S(1)} %get-tuple-element.47.ca_ref, f32[64,256]{1,0:T(8,128)S(1)} %get-tuple-element.48.sa_ref, f32[64,256]{1,0:T(8,128)S(1)} %get-tuple-element.40.cb_ref, f32[64,256]{1,0:T(8,128)S(1)} %get-tuple-element.39.sb_ref, ...), custom_call_target="tpu_custom_call" | custom-call | flops 6291456 | bytes 4194304 | tf_op jit(solution)/shard_map/tables/pallas_call | solution.py:151
  26.4 0.0 copy-start
  26.5 1.3 %copy-done = bf16[4096,256]{1,0:T(8,128)(2,1)} copy-done((bf16[4096,256]{1,0:T(8,128)(2,1)}, bf16[4096,256]{1,0:T(8,128)(2,1)S(1)}, u32[]{:S(2)}) %copy-start) | copy-done | bytes 2097176
  27.8 0.0 copy-start.1
  27.8 1.3 %copy-done.1 = bf16[256,4096]{1,0:T(8,128)(2,1)} copy-done((bf16[256,4096]{1,0:T(8,128)(2,1)}, bf16[256,4096]{1,0:T(8,128)(2,1)S(1)}, u32[]{:S(2)}) %copy-start.1) | copy-done | bytes 2097176
  29.1 0.0 copy-done.2
  29.1 0.0 copy-done.3
  29.1 0.0 copy-done.4
  29.1 0.1 multiply_multiply_fusion
  29.2 1.3 %collective-permute-start = (f32[2,2,2048]{2,1,0:T(2,128)S(1)}, f32[2,2,2048]{2,1,0:T(2,128)S(1)}, u32[]{:S(2)}, u32[]{:S(2)}) collective-permute-start(f32[2,2,2048]{2,1,0:T(2,128)S(1)} %multiply_multiply_fusion), channel_id=1, source_target_pairs={{0,32},{32,0},{64,96},{96,64},{128,160},{160,128},{192,224},{224,1... | collective-permute-start | bytes 98312 | tf_op jit(solution)/shard_map/ppermute | solution.py:355
  30.5 2.4 %collective-permute-start.1 = (f32[2,2,2048]{2,1,0:T(2,128)S(1)}, f32[2,2,2048]{2,1,0:T(2,128)S(1)}, u32[]{:S(2)}, u32[]{:S(2)}) collective-permute-start(f32[2,2,2048]{2,1,0:T(2,128)S(1)} %multiply_multiply_fusion), channel_id=1, source_target_pairs={{0,64},{32,96},{64,0},{96,32},{128,192},{160,224},{192,128},{224,1... | collective-permute-start | bytes 98312 | tf_op jit(solution)/shard_map/ppermute | solution.py:355
  32.9 0.2 collective-permute-start.2
  33.1 0.1 reshape.204
  33.3 0.1 convert_element_type.70
  33.4 0.0 copy-done.6
  33.4 0.1 fusion.25
  33.5 0.1 sine_multiply_fusion.1
  33.6 0.1 fusion.29
  33.7 0.1 copy.16.turn_ref
  33.8 0.1 broadcast_in_dim_tile.3.parity_ref
  33.9 0.0 collective-permute-done
  33.9 1.3 %collective-permute-done.1 = f32[2,2,2048]{2,1,0:T(2,128)S(1)} collective-permute-done((f32[2,2,2048]{2,1,0:T(2,128)S(1)}, f32[2,2,2048]{2,1,0:T(2,128)S(1)}, u32[]{:S(2)}, u32[]{:S(2)}) %collective-permute-start.1) | collective-permute-done | bytes 32800 | tf_op jit(solution)/shard_map/ppermute | solution.py:355
  35.2 2.0 %collective-permute-done.2 = f32[2,2,2048]{2,1,0:T(2,128)S(1)} collective-permute-done((f32[2,2,2048]{2,1,0:T(2,128)S(1)}, f32[2,2,2048]{2,1,0:T(2,128)S(1)}, u32[]{:S(2)}, u32[]{:S(2)}) %collective-permute-start.2) | collective-permute-done | bytes 32800 | tf_op jit(solution)/shard_map/ppermute | solution.py:355
  37.2 0.1 pad_maximum_fusion.near_ref
  37.3 13.1 %all-to-all-done.in_ref = bf16[32,8,16,128]{3,2,1,0:T(8,128)(2,1)S(1)} async-done(((bf16[32,8,16,128]{3,2,1,0:T(8,128)(2,1)}), bf16[32,8,16,128]{3,2,1,0:T(8,128)(2,1)S(1)}, u32[]{:S(2)}, u32[]{:S(2)}) %all-to-all-start) | async-done | bytes 1048608 | tf_op jit(solution)/shard_map/all_to_all | solution.py:366
  50.4 1.2 %collective-permute-start.3 = (f32[4,2,2,2048]{3,2,1,0:T(2,128)S(1)}, f32[4,2,2,2048]{3,2,1,0:T(2,128)S(1)}, u32[]{:S(2)}, u32[]{:S(2)}) collective-permute-start(f32[4,2,2,2048]{3,2,1,0:T(2,128)S(1)} %pad_maximum_fusion.near_ref), channel_id=1, source_target_pairs={{0,128},{32,160},{64,192},{96,224},{128,0},{160,32},{192,64},{224,... | collective-permute-start | bytes 393224 | tf_op jit(solution)/shard_map/ppermute | solution.py:355
  51.6 12.1 %cells.1 = bf16[8,32,16,128]{3,2,1,0:T(8,128)(2,1)} custom-call(bf16[32,8,16,128]{3,2,1,0:T(8,128)(2,1)S(1)} %all-to-all-done.in_ref, bf16[4096,256]{1,0:T(8,128)(2,1)} %copy-done, bf16[256,4096]{1,0:T(8,128)(2,1)} %copy-done.1, f32[256,4]{1,0:T(8,128)S(1)} %copy.16.turn_ref, f32[1,128]{1,0:T(1,128)S(1)} %broadcast_in_dim_tile.3.parity_ref), custom_call_target="tpu_custom_call" | custom-call | flops 8589934592 | bytes 8388608 | tf_op jit(solution)/shard_map/cells/pallas_call | solution.py:228
  63.7 0.0 collective-permute-done.3.far_ref
  63.7 7.6 %all-to-all-start.1 = ((bf16[256,16,128]{2,1,0:T(8,128)(2,1)}), bf16[256,16,128]{2,1,0:T(8,128)(2,1)S(1)}, u32[]{:S(2)}, u32[]{:S(2)}) async-start(bf16[256,16,128]{2,1,0:T(8,128)(2,1)} %bitcast.6), calls=%async_computation.1 | async-start | bytes 2097152 | tf_op jit(solution)/shard_map/all_to_all | solution.py:378
  71.3 0.1 pad_add_fusion.place_ref
  71.3 32.0 %all-to-all-done.1 = bf16[256,16,128]{2,1,0:T(8,128)(2,1)S(1)} async-done(((bf16[256,16,128]{2,1,0:T(8,128)(2,1)}), bf16[256,16,128]{2,1,0:T(8,128)(2,1)S(1)}, u32[]{:S(2)}, u32[]{:S(2)}) %all-to-all-start.1) | async-done | bytes 1048608 | tf_op jit(solution)/shard_map/all_to_all | solution.py:378
  103.4 6.8 %backward.1 = f32[4,4,2,2048]{3,2,1,0:T(2,128)} custom-call(s32[2]{0:T(128)S(1)} %pad_add_fusion.place_ref, bf16[8,32,16,128]{3,2,1,0:T(8,128)(2,1)S(1)} %bitcast.9, f32[4,2,2,2048]{3,2,1,0:T(2,128)S(1)} %pad_maximum_fusion.near_ref, f32[4,2,2,2048]{3,2,1,0:T(2,128)S(1)} %collective-permute-done.3.far_ref, bf16[4,2048,512]{2,1,0:T(8,128)(2,1)} %leg_ref.3), custom_call_target="tpu_custom_call" | custom-call | flops 2147483648 | bytes 10485760 | tf_op jit(solution)/shard_map/backward/pallas_call | solution.py:323
  (8 shorter events, 0.1 us)
Async XLA Ops:
  8.5 13.0 %copy-start.5 = (s32[128]{0:T(128)S(1)}, s32[128]{0:T(128)}, u32[]{:S(2)}) copy-start(s32[128]{0:T(128)} %param.11) | copy-start | bytes 1540
  8.5 20.6 %copy-start.2 = (f32[2,2,2048]{2,1,0:T(2,128)S(1)}, f32[2,2,2048]{2,1,0:T(2,128)}, u32[]{:S(2)}) copy-start(f32[2,2,2048]{2,1,0:T(2,128)} %radial_ref.1) | copy-start | bytes 98308
  8.5 20.6 %copy-start.3 = (f32[2]{0:T(128)S(1)}, f32[2]{0:T(128)}, u32[]{:S(2)}) copy-start(f32[2]{0:T(128)} %param.9) | copy-start | bytes 28
  8.5 20.6 %copy-start.4 = (f32[2]{0:T(128)S(1)}, f32[2]{0:T(128)}, u32[]{:S(2)}) copy-start(f32[2]{0:T(128)} %constant.120.clone) | copy-start | bytes 28
  8.5 24.8 %copy-start.6 = (s32[16]{0:T(128)S(1)}, s32[16]{0:T(128)}, u32[]{:S(2)}) copy-start(s32[16]{0:T(128)} %param.12) | copy-start | bytes 196
  8.6 41.8 %all-to-all-start = ((bf16[32,8,16,128]{3,2,1,0:T(8,128)(2,1)}), bf16[32,8,16,128]{3,2,1,0:T(8,128)(2,1)S(1)}, u32[]{:S(2)}, u32[]{:S(2)}) async-start(bf16[32,8,16,128]{3,2,1,0:T(8,128)(2,1)} %forward.1), calls=%async_computation | async-start | bytes 2097152 | tf_op jit(solution)/shard_map/all_to_all | solution.py:366
  26.4 1.3 %copy-start = (bf16[4096,256]{1,0:T(8,128)(2,1)}, bf16[4096,256]{1,0:T(8,128)(2,1)S(1)}, u32[]{:S(2)}) copy-start(bf16[4096,256]{1,0:T(8,128)(2,1)S(1)} %get-tuple-element.25.synth_ref) | copy-start | bytes 6291460
  27.8 1.3 %copy-start.1 = (bf16[256,4096]{1,0:T(8,128)(2,1)}, bf16[256,4096]{1,0:T(8,128)(2,1)S(1)}, u32[]{:S(2)}) copy-start(bf16[256,4096]{1,0:T(8,128)(2,1)S(1)} %get-tuple-element.26.analysis_ref) | copy-start | bytes 6291460
  29.2 4.7 %collective-permute-start = (f32[2,2,2048]{2,1,0:T(2,128)S(1)}, f32[2,2,2048]{2,1,0:T(2,128)S(1)}, u32[]{:S(2)}, u32[]{:S(2)}) collective-permute-start(f32[2,2,2048]{2,1,0:T(2,128)S(1)} %multiply_multiply_fusion), channel_id=1, source_target_pairs={{0,32},{32,0},{64,96},{96,64},{128,160},{160,128},{192,224},{224,1... | collective-permute-start | bytes 98312 | tf_op jit(solution)/shard_map/ppermute | solution.py:355
  30.5 4.7 %collective-permute-start.1 = (f32[2,2,2048]{2,1,0:T(2,128)S(1)}, f32[2,2,2048]{2,1,0:T(2,128)S(1)}, u32[]{:S(2)}, u32[]{:S(2)}) collective-permute-start(f32[2,2,2048]{2,1,0:T(2,128)S(1)} %multiply_multiply_fusion), channel_id=1, source_target_pairs={{0,64},{32,96},{64,0},{96,32},{128,192},{160,224},{192,128},{224,1... | collective-permute-start | bytes 98312 | tf_op jit(solution)/shard_map/ppermute | solution.py:355
  32.9 4.3 %collective-permute-start.2 = (f32[2,2,2048]{2,1,0:T(2,128)S(1)}, f32[2,2,2048]{2,1,0:T(2,128)S(1)}, u32[]{:S(2)}, u32[]{:S(2)}) collective-permute-start(f32[2,2,2048]{2,1,0:T(2,128)S(1)} %multiply_multiply_fusion), channel_id=1, source_target_pairs={{0,96},{32,64},{64,32},{96,0},{128,224},{160,192},{192,160},{224,1... | collective-permute-start | bytes 98312 | tf_op jit(solution)/shard_map/ppermute | solution.py:355
  50.4 13.3 %collective-permute-start.3 = (f32[4,2,2,2048]{3,2,1,0:T(2,128)S(1)}, f32[4,2,2,2048]{3,2,1,0:T(2,128)S(1)}, u32[]{:S(2)}, u32[]{:S(2)}) collective-permute-start(f32[4,2,2,2048]{3,2,1,0:T(2,128)S(1)} %pad_maximum_fusion.near_ref), channel_id=1, source_target_pairs={{0,128},{32,160},{64,192},{96,224},{128,0},{160,32},{192,64},{224,... | collective-permute-start | bytes 393224 | tf_op jit(solution)/shard_map/ppermute | solution.py:355
  63.7 39.7 %all-to-all-start.1 = ((bf16[256,16,128]{2,1,0:T(8,128)(2,1)}), bf16[256,16,128]{2,1,0:T(8,128)(2,1)S(1)}, u32[]{:S(2)}, u32[]{:S(2)}) async-start(bf16[256,16,128]{2,1,0:T(8,128)(2,1)} %bitcast.6), calls=%async_computation.1 | async-start | bytes 2097152 | tf_op jit(solution)/shard_map/all_to_all | solution.py:378

commit v3 on v2

--- a/solution.py
+++ b/solution.py
@@ -109,13 +109,7 @@
     )(harmonics, radial, legendre)
 
 
-def table_kernel(ca_ref, sa_ref, cb_ref, sb_ref, cat_ref, sat_ref, cbt_ref, sbt_ref, out_ref, flip_ref):
-    high = ca_ref.shape[0]
-    low = cb_ref.shape[0]
-    for a in range(high):
-        out_ref[a * low : (a + 1) * low, :] = (
-            ca_ref[a : a + 1, :] * cb_ref[...] - sa_ref[a : a + 1, :] * sb_ref[...]
-        ).astype(BF16)
+def table_kernel(cat_ref, sat_ref, cbt_ref, sbt_ref, flip_ref):
     wide = cbt_ref.shape[1]
     for a in range(cat_ref.shape[1]):
         flip_ref[:, a * wide : (a + 1) * wide] = (
@@ -148,18 +142,16 @@
         rows[:, None] * jnp.arange(wide, dtype=jnp.int32)[None] + shift[:, None], pixels
     )
     count = rows.shape[0]
-    return pl.pallas_call(
+    flipped = pl.pallas_call(
         table_kernel,
-        out_shape=[
-            jax.ShapeDtypeStruct((pixels, count), BF16),
-            jax.ShapeDtypeStruct((count, pixels), BF16),
-        ],
+        out_shape=jax.ShapeDtypeStruct((count, pixels), BF16),
         compiler_params=pltpu.CompilerParams(vmem_limit_bytes=24 * 2**20),
         cost_estimate=pl.CostEstimate(
-            flops=6 * pixels * count, bytes_accessed=4 * pixels * count, transcendentals=0
+            flops=3 * pixels * count, bytes_accessed=2 * pixels * count, transcendentals=0
         ),
         name="tables",
-    )(ca, sa, cb, sb, cat, sat, cbt, sbt)
+    )(cat, sat, cbt, sbt)
+    return (ca, sa), (cb, sb), flipped
 
 
 def rotation(order_table, pixels):
@@ -172,12 +164,13 @@
     return jnp.stack(columns, 1)
 
 
-def cell_kernel(in_ref, synth_ref, analysis_ref, turn_ref, parity_ref, out_ref, products, synth, analysis, sems, *, block):
+def cell_kernel(
+    in_ref, ca_ref, sa_ref, cb_ref, sb_ref, analysis_ref, turn_ref, parity_ref, out_ref, products, synth, analysis, sem, *, block
+):
     count, pixels = analysis_ref.shape
-    fetch_synth = pltpu.make_async_copy(synth_ref, synth, sems.at[0])
-    fetch_analysis = pltpu.make_async_copy(analysis_ref, analysis, sems.at[1])
-    fetch_synth.start()
+    fetch_analysis = pltpu.make_async_copy(analysis_ref, analysis, sem)
     fetch_analysis.start()
+    low = cb_ref.shape[0]
     groups = in_ref.shape[1]
     step = products.shape[1] // (2 * LANES)
     width = step * LANES
@@ -190,8 +183,7 @@
     back_sin = rot_sin * scale
 
     def swap(x):
-        grouped = x.reshape(count // 8, 8, LANES)
-        return jnp.concatenate([grouped[:, 4:], grouped[:, :4]], 1).reshape(count, LANES)
+        return pltpu.roll(x.reshape(count // 8, 8, LANES), 4, 1).reshape(count, LANES)
 
     for first in range(0, groups, step):
         turned = [[], []]
@@ -201,9 +193,12 @@
                 x = arrived[:, f * 8 : (f + 1) * 8, :].reshape(count, LANES)
                 turned[f].append((rot_cos * x + rot_sin * swap(x)).astype(BF16))
         turned = jnp.concatenate(turned[0] + turned[1], 1)
-        if first == 0:
-            fetch_synth.wait()
         for j in range(0, pixels, block):
+            if first == 0:
+                for a in range(j // low, (j + block) // low):
+                    synth[a * low : (a + 1) * low, :] = (
+                        ca_ref[a : a + 1, :] * cb_ref[...] - sa_ref[a : a + 1, :] * sb_ref[...]
+                    ).astype(BF16)
             fields = jnp.dot(synth[j : j + block, :], turned, preferred_element_type=F32)
             alpha, beta = fields[:, :width], fields[:, width:]
             products[j : j + block, :width] = (beta * beta).astype(BF16)
@@ -220,21 +215,21 @@
             out_ref[first + g] = jnp.concatenate(parts, 1).astype(BF16)
 
 
-def cells(arrived, synth, analysis, turn, parity, step=4, block=512):
+def cells(arrived, high, low, analysis, turn, parity, step=4, block=1024):
     owners, groups, rows, lanes = arrived.shape
-    pixels, count = synth.shape
+    count, pixels = analysis.shape
     whole = pl.BlockSpec(memory_space=pltpu.VMEM)
     anywhere = pl.BlockSpec(memory_space=pltpu.HBM)
     return pl.pallas_call(
         functools.partial(cell_kernel, block=block),
-        in_specs=[whole, anywhere, anywhere, whole, whole],
+        in_specs=[*[whole] * 5, anywhere, whole, whole],
         out_specs=whole,
         out_shape=jax.ShapeDtypeStruct((groups, owners, rows, lanes), BF16),
         scratch_shapes=[
             pltpu.VMEM((pixels, 2 * step * lanes), BF16),
             pltpu.VMEM((pixels, count), BF16),
             pltpu.VMEM((count, pixels), BF16),
-            pltpu.SemaphoreType.DMA((2,)),
+            pltpu.SemaphoreType.DMA,
         ],
         compiler_params=pltpu.CompilerParams(vmem_limit_bytes=50 * 2**20),
         cost_estimate=pl.CostEstimate(
@@ -243,7 +238,7 @@
             transcendentals=0,
         ),
         name="cells",
-    )(arrived, synth, analysis, turn, parity)
+    )(arrived, *high, *low, analysis, turn, parity)
 
 
 def backward_kernel(
@@ -366,13 +361,13 @@
     arrived = lax.all_to_all(outgoing, "sht", 0, 0, tiled=True)
     parity = jnp.tile(((cycle_table - NSIDE + 1) % 2).astype(F32), 8)[None]
     turn = rotation(order_table, pixels)
-    synth, analysis = tables(order_table, pixels)
-    radial, synth = lax.optimization_barrier((radial, synth))
+    high, low, analysis = tables(order_table, pixels)
+    radial, analysis = lax.optimization_barrier((radial, analysis))
     profile = radial * node_weight[:, None, None] * jnp.array([2.0, 4.0], F32)[None, :, None]
     near = jnp.stack([profile] + [swapped(profile, bit) for bit in (1, 2, 3)])
     arrived, near = lax.optimization_barrier((arrived, near))
     far = swapped(near, 4)
-    returning = cells(arrived, synth, analysis, turn, parity)
+    returning = cells(arrived, high, low, analysis, turn, parity)
     returning, far = lax.optimization_barrier((returning, far))
     returning = returning.reshape(groups * owners, 16, LANES)
     at_orders = lax.all_to_all(returning, ("node", "sht"), 0, 0, tiled=True)

time: 111 us -> 111 us (level)
  waiting for transfers between devices: 48.4 us -> 50.2 us
  local copies, waits for them, and re-layouts: 3.53 us -> 2.22 us
    all_to_all x1, waiting for transfers between devices: 13.1 us -> 15.4 us  [on_device(): arrived = lax.all_to_all(outgoing, 'sht', 0, 0, tiled=True)]
    unnamed x14 -> x12, local copies, waits for them, and re-layouts: 2.66 us -> 1.35 us
where the time goes in v3:
time: 111 us; the launch traced here: 110 us
  waiting for transfers between devices  50.2 us (45%)
  Pallas kernels  29.8 us (27%)
  starting transfers between devices  25.5 us (23%)
  other arithmetic  2.24 us (2%)
  local copies, waits for them, and re-layouts  2.22 us (2%)
    all_to_all x1, waiting for transfers between devices, on_device(): at_orders = lax.all_to_all(returning, ('node', 'sht'), 0, 0, tiled=True)  32 us
    all_to_all x1, waiting for transfers between devices, on_device(): arrived = lax.all_to_all(outgoing, 'sht', 0, 0, tiled=True)  15.4 us
    all_to_all x1, starting transfers between devices, on_device(): arrived = lax.all_to_all(outgoing, 'sht', 0, 0, tiled=True)  12.8 us
    pallas_call x1, Pallas kernels, cells(): pl.pallas_call(functools.partial(cell_kernel, block=block), in_specs=[*[w...  11.8 us
    pallas_call x1, Pallas kernels, forward(): pl.pallas_call(forward_kernel, grid=(orders_dev,), in_specs=[pl.BlockSpec...  8.9 us
    all_to_all x1, starting transfers between devices, on_device(): at_orders = lax.all_to_all(returning, ('node', 'sht'), 0, 0, tiled=True)  7.56 us
    pallas_call x1, Pallas kernels, backward(): pl.pallas_call(backward_kernel, grid_spec=pltpu.PrefetchScalarGridSpec(nu...  6.77 us
    ppermute x4, starting transfers between devices, swapped(): lax.ppermute(value, 'node', [(i, i ^ bit) for i in range(lax.axis_size('n...  5.17 us
  transfers between devices with their start and end apart: 6, of which 4 were waited for; matrix products, arithmetic and copies ran while one was open for 3% of the time, Pallas kernels for 13%

profile of v3, /device:TPU:1, one launch (start us, length us, event | category | flops | bytes accessed | tf_op | source)
XLA Modules:
  0.0 110.3 jit_solution(17670793731007291724)
XLA Ops:
  0.0 0.0 copy-start.3
  0.0 0.0 copy-start.1
  0.0 0.0 copy-start.4
  0.0 0.0 copy-start.5
  0.0 0.0 copy-start.2
  0.0 8.9 %forward.1 = bf16[32,8,16,128]{3,2,1,0:T(8,128)(2,1)} custom-call(bf16[4,32,2,2048]{3,2,1,0:T(2,128)(2,1)} %harm_ref.1, f32[2,2,2048]{2,1,0:T(2,128)} %radial_ref.1, bf16[4,2048,512]{2,1,0:T(8,128)(2,1)} %leg_ref.3), custom_call_target="tpu_custom_call" | custom-call | flops 2147483648 | bytes 10485760 | tf_op jit(solution)/shard_map/forward/pallas_call | solution.py:88
  8.9 12.8 %all-to-all-start = ((bf16[32,8,16,128]{3,2,1,0:T(8,128)(2,1)}), bf16[32,8,16,128]{3,2,1,0:T(8,128)(2,1)S(1)}, u32[]{:S(2)}, u32[]{:S(2)}) async-start(bf16[32,8,16,128]{3,2,1,0:T(8,128)(2,1)} %forward.1), calls=%async_computation | async-start | bytes 2097152 | tf_op jit(solution)/shard_map/all_to_all | solution.py:361
  21.7 0.0 copy-done.4
  21.7 0.1 broadcast_in_dim.12
  21.8 0.1 mul.207
  22.0 0.1 mul.220
  22.1 0.6 fusion.3
  22.7 0.1 fusion.13
  22.8 0.1 copy.15
  22.9 0.5 multiply_sine_fusion
  23.4 2.3 %tables.1.analysis_ref = bf16[256,4096]{1,0:T(8,128)(2,1)S(1)} custom-call(f32[256,32]{1,0:T(8,128)S(1)} %get-tuple-element.32.cat_ref, f32[256,32]{1,0:T(8,128)S(1)} %get-tuple-element.31.sat_ref, f32[256,128]{1,0:T(8,128)S(1)} %get-tuple-element.36.cbt_ref, f32[256,128]{1,0:T(8,128)S(1)} %get-tuple-element.35.sbt_ref), custom_call_target="tpu_custom_call" | custom-call | flops 3145728 | bytes 2097152 | tf_op jit(solution)/shard_map/tables/pallas_call | solution.py:145
  25.7 0.0 copy-start
  25.7 1.3 %copy-done = bf16[256,4096]{1,0:T(8,128)(2,1)} copy-done((bf16[256,4096]{1,0:T(8,128)(2,1)}, bf16[256,4096]{1,0:T(8,128)(2,1)S(1)}, u32[]{:S(2)}) %copy-start) | copy-done | bytes 2097176
  27.0 0.0 copy-done.3
  27.0 0.0 copy-done.1
  27.0 0.0 copy-done.2
  27.0 0.1 multiply_multiply_fusion
  27.1 1.3 %collective-permute-start = (f32[2,2,2048]{2,1,0:T(2,128)S(1)}, f32[2,2,2048]{2,1,0:T(2,128)S(1)}, u32[]{:S(2)}, u32[]{:S(2)}) collective-permute-start(f32[2,2,2048]{2,1,0:T(2,128)S(1)} %multiply_multiply_fusion), channel_id=1, source_target_pairs={{0,32},{32,0},{64,96},{96,64},{128,160},{160,128},{192,224},{224,1... | collective-permute-start | bytes 98312 | tf_op jit(solution)/shard_map/ppermute | solution.py:350
  28.4 2.4 %collective-permute-start.1 = (f32[2,2,2048]{2,1,0:T(2,128)S(1)}, f32[2,2,2048]{2,1,0:T(2,128)S(1)}, u32[]{:S(2)}, u32[]{:S(2)}) collective-permute-start(f32[2,2,2048]{2,1,0:T(2,128)S(1)} %multiply_multiply_fusion), channel_id=1, source_target_pairs={{0,64},{32,96},{64,0},{96,32},{128,192},{160,224},{192,128},{224,1... | collective-permute-start | bytes 98312 | tf_op jit(solution)/shard_map/ppermute | solution.py:350
  30.8 0.2 collective-permute-start.2
  31.0 0.1 reshape.204
  31.2 0.1 convert_element_type.70
  31.3 0.0 copy-done.5
  31.3 0.1 fusion.25
  31.4 0.1 sine_multiply_fusion.1
  31.5 0.5 fusion.11
  32.0 0.1 fusion.29
  32.1 0.1 copy.16.turn_ref
  32.3 0.1 broadcast_in_dim_tile.3.parity_ref
  32.4 0.0 collective-permute-done
  32.4 0.8 collective-permute-done.1
  33.1 2.0 %collective-permute-done.2 = f32[2,2,2048]{2,1,0:T(2,128)S(1)} collective-permute-done((f32[2,2,2048]{2,1,0:T(2,128)S(1)}, f32[2,2,2048]{2,1,0:T(2,128)S(1)}, u32[]{:S(2)}, u32[]{:S(2)}) %collective-permute-start.2) | collective-permute-done | bytes 32800 | tf_op jit(solution)/shard_map/ppermute | solution.py:350
  35.1 0.1 pad_maximum_fusion.near_ref
  35.2 15.4 %all-to-all-done.in_ref = bf16[32,8,16,128]{3,2,1,0:T(8,128)(2,1)S(1)} async-done(((bf16[32,8,16,128]{3,2,1,0:T(8,128)(2,1)}), bf16[32,8,16,128]{3,2,1,0:T(8,128)(2,1)S(1)}, u32[]{:S(2)}, u32[]{:S(2)}) %all-to-all-start) | async-done | bytes 1048608 | tf_op jit(solution)/shard_map/all_to_all | solution.py:361
  50.6 1.2 %collective-permute-start.3 = (f32[4,2,2,2048]{3,2,1,0:T(2,128)S(1)}, f32[4,2,2,2048]{3,2,1,0:T(2,128)S(1)}, u32[]{:S(2)}, u32[]{:S(2)}) collective-permute-start(f32[4,2,2,2048]{3,2,1,0:T(2,128)S(1)} %pad_maximum_fusion.near_ref), channel_id=1, source_target_pairs={{0,128},{32,160},{64,192},{96,224},{128,0},{160,32},{192,64},{224,... | collective-permute-start | bytes 393224 | tf_op jit(solution)/shard_map/ppermute | solution.py:350
  51.8 11.8 %cells.1 = bf16[8,32,16,128]{3,2,1,0:T(8,128)(2,1)} custom-call(bf16[32,8,16,128]{3,2,1,0:T(8,128)(2,1)S(1)} %all-to-all-done.in_ref, f32[64,256]{1,0:T(8,128)S(1)} %get-tuple-element.43.ca_ref, f32[64,256]{1,0:T(8,128)S(1)} %get-tuple-element.44.sa_ref, f32[64,256]{1,0:T(8,128)S(1)} %get-tuple-element.34.cb_ref, f32[64,256]{1,0:T(8,128)S(1)} %get-tuple-element.33.sb_ref, ...), custom_call_target="tpu_custom_call" | custom-call | flops 8589934592 | bytes 8388608 | tf_op jit(solution)/shard_map/cells/pallas_call | solution.py:223
  63.6 0.0 collective-permute-done.3.far_ref
  63.7 7.6 %all-to-all-start.1 = ((bf16[256,16,128]{2,1,0:T(8,128)(2,1)}), bf16[256,16,128]{2,1,0:T(8,128)(2,1)S(1)}, u32[]{:S(2)}, u32[]{:S(2)}) async-start(bf16[256,16,128]{2,1,0:T(8,128)(2,1)} %bitcast.6), calls=%async_computation.1 | async-start | bytes 2097152 | tf_op jit(solution)/shard_map/all_to_all | solution.py:373
  71.3 0.1 pad_add_fusion.place_ref
  71.3 32.0 %all-to-all-done.1 = bf16[256,16,128]{2,1,0:T(8,128)(2,1)S(1)} async-done(((bf16[256,16,128]{2,1,0:T(8,128)(2,1)}), bf16[256,16,128]{2,1,0:T(8,128)(2,1)S(1)}, u32[]{:S(2)}, u32[]{:S(2)}) %all-to-all-start.1) | async-done | bytes 1048608 | tf_op jit(solution)/shard_map/all_to_all | solution.py:373
  103.4 6.8 %backward.1 = f32[4,4,2,2048]{3,2,1,0:T(2,128)} custom-call(s32[2]{0:T(128)S(1)} %pad_add_fusion.place_ref, bf16[8,32,16,128]{3,2,1,0:T(8,128)(2,1)S(1)} %bitcast.9, f32[4,2,2,2048]{3,2,1,0:T(2,128)S(1)} %pad_maximum_fusion.near_ref, f32[4,2,2,2048]{3,2,1,0:T(2,128)S(1)} %collective-permute-done.3.far_ref, bf16[4,2048,512]{2,1,0:T(8,128)(2,1)} %leg_ref.3), custom_call_target="tpu_custom_call" | custom-call | flops 2147483648 | bytes 10485760 | tf_op jit(solution)/shard_map/backward/pallas_call | solution.py:318
  (8 shorter events, 0.1 us)
Async XLA Ops:
  0.0 27.0 %copy-start.3 = (f32[2]{0:T(128)S(1)}, f32[2]{0:T(128)}, u32[]{:S(2)}) copy-start(f32[2]{0:T(128)} %constant.120.clone) | copy-start | bytes 28
  0.0 27.0 %copy-start.1 = (f32[2,2,2048]{2,1,0:T(2,128)S(1)}, f32[2,2,2048]{2,1,0:T(2,128)}, u32[]{:S(2)}) copy-start(f32[2,2,2048]{2,1,0:T(2,128)} %radial_ref.1) | copy-start | bytes 98308
  0.0 21.7 %copy-start.4 = (s32[128]{0:T(128)S(1)}, s32[128]{0:T(128)}, u32[]{:S(2)}) copy-start(s32[128]{0:T(128)} %param.11) | copy-start | bytes 1540
  0.0 31.3 %copy-start.5 = (s32[16]{0:T(128)S(1)}, s32[16]{0:T(128)}, u32[]{:S(2)}) copy-start(s32[16]{0:T(128)} %param.12) | copy-start | bytes 196
  0.0 27.0 %copy-start.2 = (f32[2]{0:T(128)S(1)}, f32[2]{0:T(128)}, u32[]{:S(2)}) copy-start(f32[2]{0:T(128)} %param.9) | copy-start | bytes 28
  8.9 41.7 %all-to-all-start = ((bf16[32,8,16,128]{3,2,1,0:T(8,128)(2,1)}), bf16[32,8,16,128]{3,2,1,0:T(8,128)(2,1)S(1)}, u32[]{:S(2)}, u32[]{:S(2)}) async-start(bf16[32,8,16,128]{3,2,1,0:T(8,128)(2,1)} %forward.1), calls=%async_computation | async-start | bytes 2097152 | tf_op jit(solution)/shard_map/all_to_all | solution.py:361
  25.7 1.3 %copy-start = (bf16[256,4096]{1,0:T(8,128)(2,1)}, bf16[256,4096]{1,0:T(8,128)(2,1)S(1)}, u32[]{:S(2)}) copy-start(bf16[256,4096]{1,0:T(8,128)(2,1)S(1)} %tables.1.analysis_ref) | copy-start | bytes 6291460
  27.1 5.3 %collective-permute-start = (f32[2,2,2048]{2,1,0:T(2,128)S(1)}, f32[2,2,2048]{2,1,0:T(2,128)S(1)}, u32[]{:S(2)}, u32[]{:S(2)}) collective-permute-start(f32[2,2,2048]{2,1,0:T(2,128)S(1)} %multiply_multiply_fusion), channel_id=1, source_target_pairs={{0,32},{32,0},{64,96},{96,64},{128,160},{160,128},{192,224},{224,1... | collective-permute-start | bytes 98312 | tf_op jit(solution)/shard_map/ppermute | solution.py:350
  28.4 4.7 %collective-permute-start.1 = (f32[2,2,2048]{2,1,0:T(2,128)S(1)}, f32[2,2,2048]{2,1,0:T(2,128)S(1)}, u32[]{:S(2)}, u32[]{:S(2)}) collective-permute-start(f32[2,2,2048]{2,1,0:T(2,128)S(1)} %multiply_multiply_fusion), channel_id=1, source_target_pairs={{0,64},{32,96},{64,0},{96,32},{128,192},{160,224},{192,128},{224,1... | collective-permute-start | bytes 98312 | tf_op jit(solution)/shard_map/ppermute | solution.py:350
  30.8 4.3 %collective-permute-start.2 = (f32[2,2,2048]{2,1,0:T(2,128)S(1)}, f32[2,2,2048]{2,1,0:T(2,128)S(1)}, u32[]{:S(2)}, u32[]{:S(2)}) collective-permute-start(f32[2,2,2048]{2,1,0:T(2,128)S(1)} %multiply_multiply_fusion), channel_id=1, source_target_pairs={{0,96},{32,64},{64,32},{96,0},{128,224},{160,192},{192,160},{224,1... | collective-permute-start | bytes 98312 | tf_op jit(solution)/shard_map/ppermute | solution.py:350
  50.6 13.1 %collective-permute-start.3 = (f32[4,2,2,2048]{3,2,1,0:T(2,128)S(1)}, f32[4,2,2,2048]{3,2,1,0:T(2,128)S(1)}, u32[]{:S(2)}, u32[]{:S(2)}) collective-permute-start(f32[4,2,2,2048]{3,2,1,0:T(2,128)S(1)} %pad_maximum_fusion.near_ref), channel_id=1, source_target_pairs={{0,128},{32,160},{64,192},{96,224},{128,0},{160,32},{192,64},{224,... | collective-permute-start | bytes 393224 | tf_op jit(solution)/shard_map/ppermute | solution.py:350
  63.7 39.7 %all-to-all-start.1 = ((bf16[256,16,128]{2,1,0:T(8,128)(2,1)}), bf16[256,16,128]{2,1,0:T(8,128)(2,1)S(1)}, u32[]{:S(2)}, u32[]{:S(2)}) async-start(bf16[256,16,128]{2,1,0:T(8,128)(2,1)} %bitcast.6), calls=%async_computation.1 | async-start | bytes 2097152 | tf_op jit(solution)/shard_map/all_to_all | solution.py:373

commit v4 on v3

--- a/solution.py
+++ b/solution.py
@@ -14,18 +14,17 @@
 LANES = 128
 
 
-def exchange_blocks(arrays):
-    arrays = list(arrays)
+def deal_blocks(arrays):
+    arrays = [arrays[-i % 8] for i in range(8)]
     block = lax.broadcasted_iota(jnp.int32, arrays[0].shape, 1) // 16
     for bit in (1, 2, 4):
-        low = block & bit == 0
-        for i in range(8):
-            if i & bit:
-                continue
-            a, b = arrays[i], arrays[i | bit]
-            arrays[i] = jnp.where(low, a, pltpu.roll(b, 16 * bit, 1))
-            arrays[i | bit] = jnp.where(low, pltpu.roll(a, LANES - 16 * bit, 1), b)
+        moved = block & bit != 0
+        arrays = [jnp.where(moved, arrays[(i - bit) % 8], arrays[i]) for i in range(8)]
     return arrays
+
+
+def shift_blocks(value, count):
+    return value if count == 0 else pltpu.roll(value, 16 * count, 1)
 
 
 def forward_kernel(harm_ref, radial_ref, leg_ref, out_ref, lines, staged):
@@ -75,7 +74,9 @@
     def _():
         size = groups * 16
         for lane in range(staged.shape[0]):
-            blocks = exchange_blocks([staged[lane, i * size : (i + 1) * size, :] for i in range(8)])
+            blocks = deal_blocks(
+                [shift_blocks(staged[lane, i * size : (i + 1) * size, :], i) for i in range(8)]
+            )
             for i in range(8):
                 out_ref[lane * 8 + i] = blocks[i].astype(BF16).reshape(groups, 16, LANES)
 
@@ -260,12 +261,13 @@
             fetch(o).start()
 
         def chunk(lane, carry):
-            blocks = exchange_blocks(
+            blocks = deal_blocks(
                 [
                     in_ref[:, lane * per + i].astype(F32).reshape(sources * 16, LANES)
                     for i in range(per)
                 ]
             )
+            blocks = [shift_blocks(block, -i % per) for i, block in enumerate(blocks)]
             for i in range(per):
                 for group in range(sources):
                     staged[lane, pl.ds((group * per + i) * 16, 16), :] = blocks[i][
@@ -365,7 +367,6 @@
     radial, analysis = lax.optimization_barrier((radial, analysis))
     profile = radial * node_weight[:, None, None] * jnp.array([2.0, 4.0], F32)[None, :, None]
     near = jnp.stack([profile] + [swapped(profile, bit) for bit in (1, 2, 3)])
-    arrived, near = lax.optimization_barrier((arrived, near))
     far = swapped(near, 4)
     returning = cells(arrived, high, low, analysis, turn, parity)
     returning, far = lax.optimization_barrier((returning, far))

time: 111 us -> 109 us (0.982)
  no operation moved by 1% of the time
where the time goes in v4:
time: 109 us
  waiting for transfers between devices  49.9 us (46%)
  Pallas kernels  29 us (27%)
  starting transfers between devices  25.3 us (23%)
  other arithmetic  2.24 us (2%)
  local copies, waits for them, and re-layouts  2.22 us (2%)
    all_to_all x1, waiting for transfers between devices, on_device(): at_orders = lax.all_to_all(returning, ('node', 'sht'), 0, 0, tiled=True)  32 us
    all_to_all x1, waiting for transfers between devices, on_device(): arrived = lax.all_to_all(outgoing, 'sht', 0, 0, tiled=True)  15.5 us
    all_to_all x1, starting transfers between devices, on_device(): arrived = lax.all_to_all(outgoing, 'sht', 0, 0, tiled=True)  12.8 us
    pallas_call x1, Pallas kernels, cells(): pl.pallas_call(functools.partial(cell_kernel, block=block), in_specs=[*[w...  11.8 us
    pallas_call x1, Pallas kernels, forward(): pl.pallas_call(forward_kernel, grid=(orders_dev,), in_specs=[pl.BlockSpec...  8.27 us
    all_to_all x1, starting transfers between devices, on_device(): at_orders = lax.all_to_all(returning, ('node', 'sht'), 0, 0, tiled=True)  7.81 us
    pallas_call x1, Pallas kernels, backward(): pl.pallas_call(backward_kernel, grid_spec=pltpu.PrefetchScalarGridSpec(nu...  6.64 us
    ppermute x4, starting transfers between devices, swapped(): lax.ppermute(value, 'node', [(i, i ^ bit) for i in range(lax.axis_size('n...  4.71 us
  transfers between devices with their start and end apart: 6, of which 4 were waited for; matrix products, arithmetic and copies ran while one was open for 3% of the time, Pallas kernels for 13%

profile of v4, /device:TPU:1, one launch (start us, length us, event | category | flops | bytes accessed | tf_op | source)
XLA Modules:
  0.0 109.1 jit_solution(3076910745452608868)
XLA Ops:
  0.0 0.0 copy-start.3
  0.0 0.0 copy-start.1
  0.0 0.0 copy-start.5
  0.0 0.0 copy-start.4
  0.0 0.0 copy-start.2
  0.0 8.3 %forward.1 = bf16[32,8,16,128]{3,2,1,0:T(8,128)(2,1)} custom-call(bf16[4,32,2,2048]{3,2,1,0:T(2,128)(2,1)} %harm_ref.1, f32[2,2,2048]{2,1,0:T(2,128)} %radial_ref.1, bf16[4,2048,512]{2,1,0:T(8,128)(2,1)} %leg_ref.3), custom_call_target="tpu_custom_call" | custom-call | flops 2147483648 | bytes 10485760 | tf_op jit(solution)/shard_map/forward/pallas_call | solution.py:89
  8.3 12.8 %all-to-all-start = ((bf16[32,8,16,128]{3,2,1,0:T(8,128)(2,1)}), bf16[32,8,16,128]{3,2,1,0:T(8,128)(2,1)S(1)}, u32[]{:S(2)}, u32[]{:S(2)}) async-start(bf16[32,8,16,128]{3,2,1,0:T(8,128)(2,1)} %forward.1), calls=%async_computation | async-start | bytes 2097152 | tf_op jit(solution)/shard_map/all_to_all | solution.py:363
  21.1 0.1 mul.218
  21.2 0.0 copy-done.4
  21.2 0.1 broadcast_in_dim.12
  21.3 0.1 mul.210
  21.4 0.1 fusion.13
  21.5 0.1 copy.15
  21.6 0.5 multiply_sine_fusion
  22.1 0.6 fusion.3
  22.7 2.3 %tables.1.analysis_ref = bf16[256,4096]{1,0:T(8,128)(2,1)S(1)} custom-call(f32[256,32]{1,0:T(8,128)S(1)} %get-tuple-element.28.cat_ref, f32[256,32]{1,0:T(8,128)S(1)} %get-tuple-element.27.sat_ref, f32[256,128]{1,0:T(8,128)S(1)} %get-tuple-element.30.cbt_ref, f32[256,128]{1,0:T(8,128)S(1)} %get-tuple-element.29.sbt_ref), custom_call_target="tpu_custom_call" | custom-call | flops 3145728 | bytes 2097152 | tf_op jit(solution)/shard_map/tables/pallas_call | solution.py:146
  25.0 0.0 copy-start
  25.0 1.3 %copy-done = bf16[256,4096]{1,0:T(8,128)(2,1)} copy-done((bf16[256,4096]{1,0:T(8,128)(2,1)}, bf16[256,4096]{1,0:T(8,128)(2,1)S(1)}, u32[]{:S(2)}) %copy-start) | copy-done | bytes 2097176
  26.4 0.0 copy-done.3
  26.4 0.0 copy-done.1
  26.4 0.0 copy-done.2
  26.4 0.1 multiply_multiply_fusion
  26.5 2.8 %collective-permute-start.1 = (f32[2,2,2048]{2,1,0:T(2,128)S(1)}, f32[2,2,2048]{2,1,0:T(2,128)S(1)}, u32[]{:S(2)}, u32[]{:S(2)}) collective-permute-start(f32[2,2,2048]{2,1,0:T(2,128)S(1)} %multiply_multiply_fusion), channel_id=1, source_target_pairs={{0,64},{32,96},{64,0},{96,32},{128,192},{160,224},{192,128},{224,1... | collective-permute-start | bytes 98312 | tf_op jit(solution)/shard_map/ppermute | solution.py:352
  29.3 0.3 collective-permute-start
  29.6 0.6 collective-permute-start.2
  30.2 0.1 reshape.204
  30.3 0.1 convert_element_type.70
  30.4 0.0 copy-done.5
  30.4 0.1 fusion.25
  30.5 0.1 sine_multiply_fusion.1
  30.6 0.5 fusion.11
  31.2 0.1 fusion.29
  31.3 0.1 broadcast_in_dim_tile.3.parity_ref
  31.3 0.1 copy.16.turn_ref
  31.5 0.0 collective-permute-done.1
  31.5 0.8 collective-permute-done
  32.4 1.5 %collective-permute-done.2 = f32[2,2,2048]{2,1,0:T(2,128)S(1)} collective-permute-done((f32[2,2,2048]{2,1,0:T(2,128)S(1)}, f32[2,2,2048]{2,1,0:T(2,128)S(1)}, u32[]{:S(2)}, u32[]{:S(2)}) %collective-permute-start.2) | collective-permute-done | bytes 32800 | tf_op jit(solution)/shard_map/ppermute | solution.py:352
  33.9 0.1 pad_maximum_fusion.near_ref
  33.9 1.0 collective-permute-start.3
  35.0 15.5 %all-to-all-done.in_ref = bf16[32,8,16,128]{3,2,1,0:T(8,128)(2,1)S(1)} async-done(((bf16[32,8,16,128]{3,2,1,0:T(8,128)(2,1)}), bf16[32,8,16,128]{3,2,1,0:T(8,128)(2,1)S(1)}, u32[]{:S(2)}, u32[]{:S(2)}) %all-to-all-start) | async-done | bytes 1048608 | tf_op jit(solution)/shard_map/all_to_all | solution.py:363
  50.5 11.8 %cells.1 = bf16[8,32,16,128]{3,2,1,0:T(8,128)(2,1)} custom-call(bf16[32,8,16,128]{3,2,1,0:T(8,128)(2,1)S(1)} %all-to-all-done.in_ref, f32[64,256]{1,0:T(8,128)S(1)} %get-tuple-element.39.ca_ref, f32[64,256]{1,0:T(8,128)S(1)} %get-tuple-element.40.sa_ref, f32[64,256]{1,0:T(8,128)S(1)} %get-tuple-element.32.cb_ref, f32[64,256]{1,0:T(8,128)S(1)} %get-tuple-element.31.sb_ref, ...), custom_call_target="tpu_custom_call" | custom-call | flops 8589934592 | bytes 8388608 | tf_op jit(solution)/shard_map/cells/pallas_call | solution.py:224
  62.3 0.0 collective-permute-done.3.far_ref
  62.3 7.8 %all-to-all-start.1 = ((bf16[256,16,128]{2,1,0:T(8,128)(2,1)}), bf16[256,16,128]{2,1,0:T(8,128)(2,1)S(1)}, u32[]{:S(2)}, u32[]{:S(2)}) async-start(bf16[256,16,128]{2,1,0:T(8,128)(2,1)} %bitcast.6), calls=%async_computation.1 | async-start | bytes 2097152 | tf_op jit(solution)/shard_map/all_to_all | solution.py:374
  70.2 0.1 pad_add_fusion.place_ref
  70.2 32.0 %all-to-all-done.1 = bf16[256,16,128]{2,1,0:T(8,128)(2,1)S(1)} async-done(((bf16[256,16,128]{2,1,0:T(8,128)(2,1)}), bf16[256,16,128]{2,1,0:T(8,128)(2,1)S(1)}, u32[]{:S(2)}, u32[]{:S(2)}) %all-to-all-start.1) | async-done | bytes 1048608 | tf_op jit(solution)/shard_map/all_to_all | solution.py:374
  102.3 6.6 %backward.1 = f32[4,4,2,2048]{3,2,1,0:T(2,128)} custom-call(s32[2]{0:T(128)S(1)} %pad_add_fusion.place_ref, bf16[8,32,16,128]{3,2,1,0:T(8,128)(2,1)S(1)} %bitcast.9, f32[4,2,2,2048]{3,2,1,0:T(2,128)S(1)} %pad_maximum_fusion.near_ref, f32[4,2,2,2048]{3,2,1,0:T(2,128)S(1)} %collective-permute-done.3.far_ref, bf16[4,2048,512]{2,1,0:T(8,128)(2,1)} %leg_ref.3), custom_call_target="tpu_custom_call" | custom-call | flops 2147483648 | bytes 10485760 | tf_op jit(solution)/shard_map/backward/pallas_call | solution.py:320
  (8 shorter events, 0.1 us)
Async XLA Ops:
  0.0 26.4 %copy-start.3 = (f32[2]{0:T(128)S(1)}, f32[2]{0:T(128)}, u32[]{:S(2)}) copy-start(f32[2]{0:T(128)} %constant.120.clone) | copy-start | bytes 28
  0.0 26.4 %copy-start.1 = (f32[2,2,2048]{2,1,0:T(2,128)S(1)}, f32[2,2,2048]{2,1,0:T(2,128)}, u32[]{:S(2)}) copy-start(f32[2,2,2048]{2,1,0:T(2,128)} %radial_ref.1) | copy-start | bytes 98308
  0.0 30.4 %copy-start.5 = (s32[16]{0:T(128)S(1)}, s32[16]{0:T(128)}, u32[]{:S(2)}) copy-start(s32[16]{0:T(128)} %param.12) | copy-start | bytes 196
  0.0 21.2 %copy-start.4 = (s32[128]{0:T(128)S(1)}, s32[128]{0:T(128)}, u32[]{:S(2)}) copy-start(s32[128]{0:T(128)} %param.11) | copy-start | bytes 1540
  0.0 26.3 %copy-start.2 = (f32[2]{0:T(128)S(1)}, f32[2]{0:T(128)}, u32[]{:S(2)}) copy-start(f32[2]{0:T(128)} %param.9) | copy-start | bytes 28
  8.3 42.2 %all-to-all-start = ((bf16[32,8,16,128]{3,2,1,0:T(8,128)(2,1)}), bf16[32,8,16,128]{3,2,1,0:T(8,128)(2,1)S(1)}, u32[]{:S(2)}, u32[]{:S(2)}) async-start(bf16[32,8,16,128]{3,2,1,0:T(8,128)(2,1)} %forward.1), calls=%async_computation | async-start | bytes 2097152 | tf_op jit(solution)/shard_map/all_to_all | solution.py:363
  25.0 1.3 %copy-start = (bf16[256,4096]{1,0:T(8,128)(2,1)}, bf16[256,4096]{1,0:T(8,128)(2,1)S(1)}, u32[]{:S(2)}) copy-start(bf16[256,4096]{1,0:T(8,128)(2,1)S(1)} %tables.1.analysis_ref) | copy-start | bytes 6291460
  26.5 5.0 %collective-permute-start.1 = (f32[2,2,2048]{2,1,0:T(2,128)S(1)}, f32[2,2,2048]{2,1,0:T(2,128)S(1)}, u32[]{:S(2)}, u32[]{:S(2)}) collective-permute-start(f32[2,2,2048]{2,1,0:T(2,128)S(1)} %multiply_multiply_fusion), channel_id=1, source_target_pairs={{0,64},{32,96},{64,0},{96,32},{128,192},{160,224},{192,128},{224,1... | collective-permute-start | bytes 98312 | tf_op jit(solution)/shard_map/ppermute | solution.py:352
  29.3 3.1 %collective-permute-start = (f32[2,2,2048]{2,1,0:T(2,128)S(1)}, f32[2,2,2048]{2,1,0:T(2,128)S(1)}, u32[]{:S(2)}, u32[]{:S(2)}) collective-permute-start(f32[2,2,2048]{2,1,0:T(2,128)S(1)} %multiply_multiply_fusion), channel_id=1, source_target_pairs={{0,32},{32,0},{64,96},{96,64},{128,160},{160,128},{192,224},{224,1... | collective-permute-start | bytes 98312 | tf_op jit(solution)/shard_map/ppermute | solution.py:352
  29.6 4.3 %collective-permute-start.2 = (f32[2,2,2048]{2,1,0:T(2,128)S(1)}, f32[2,2,2048]{2,1,0:T(2,128)S(1)}, u32[]{:S(2)}, u32[]{:S(2)}) collective-permute-start(f32[2,2,2048]{2,1,0:T(2,128)S(1)} %multiply_multiply_fusion), channel_id=1, source_target_pairs={{0,96},{32,64},{64,32},{96,0},{128,224},{160,192},{192,160},{224,1... | collective-permute-start | bytes 98312 | tf_op jit(solution)/shard_map/ppermute | solution.py:352
  33.9 28.4 %collective-permute-start.3 = (f32[4,2,2,2048]{3,2,1,0:T(2,128)S(1)}, f32[4,2,2,2048]{3,2,1,0:T(2,128)S(1)}, u32[]{:S(2)}, u32[]{:S(2)}) collective-permute-start(f32[4,2,2,2048]{3,2,1,0:T(2,128)S(1)} %pad_maximum_fusion.near_ref), channel_id=1, source_target_pairs={{0,128},{32,160},{64,192},{96,224},{128,0},{160,32},{192,64},{224,... | collective-permute-start | bytes 393224 | tf_op jit(solution)/shard_map/ppermute | solution.py:352
  62.3 40.0 %all-to-all-start.1 = ((bf16[256,16,128]{2,1,0:T(8,128)(2,1)}), bf16[256,16,128]{2,1,0:T(8,128)(2,1)S(1)}, u32[]{:S(2)}, u32[]{:S(2)}) async-start(bf16[256,16,128]{2,1,0:T(8,128)(2,1)} %bitcast.6), calls=%async_computation.1 | async-start | bytes 2097152 | tf_op jit(solution)/shard_map/all_to_all | solution.py:374

commit v5 on v4

--- a/solution.py
+++ b/solution.py
@@ -110,12 +110,30 @@
     )(harmonics, radial, legendre)
 
 
-def table_kernel(cat_ref, sat_ref, cbt_ref, sbt_ref, flip_ref):
+def table_kernel(
+    ca_ref, sa_ref, cb_ref, sb_ref, cat_ref, sat_ref, cbt_ref, sbt_ref, out_ref, flip_ref, flip, sems
+):
     wide = cbt_ref.shape[1]
-    for a in range(cat_ref.shape[1]):
-        flip_ref[:, a * wide : (a + 1) * wide] = (
-            cat_ref[:, a : a + 1] * cbt_ref[...] - sat_ref[:, a : a + 1] * sbt_ref[...]
+    pieces = sems.shape[0]
+    per = cat_ref.shape[1] // pieces
+    copies = []
+    for piece in range(pieces):
+        for a in range(piece * per, (piece + 1) * per):
+            flip[:, a * wide : (a + 1) * wide] = (
+                cat_ref[:, a : a + 1] * cbt_ref[...] - sat_ref[:, a : a + 1] * sbt_ref[...]
+            ).astype(BF16)
+        columns = pl.ds(piece * per * wide, per * wide)
+        copies.append(
+            pltpu.make_async_copy(flip.at[:, columns], flip_ref.at[:, columns], sems.at[piece])
+        )
+        copies[-1].start()
+    low = cb_ref.shape[0]
+    for a in range(ca_ref.shape[0]):
+        out_ref[a * low : (a + 1) * low, :] = (
+            ca_ref[a : a + 1, :] * cb_ref[...] - sa_ref[a : a + 1, :] * sb_ref[...]
         ).astype(BF16)
+    for copy in copies:
+        copy.wait()
 
 
 def angle(index, period):
@@ -143,16 +161,20 @@
         rows[:, None] * jnp.arange(wide, dtype=jnp.int32)[None] + shift[:, None], pixels
     )
     count = rows.shape[0]
-    flipped = pl.pallas_call(
+    return pl.pallas_call(
         table_kernel,
-        out_shape=jax.ShapeDtypeStruct((count, pixels), BF16),
+        out_specs=[pl.BlockSpec(memory_space=pltpu.VMEM), pl.BlockSpec(memory_space=pltpu.HBM)],
+        out_shape=[
+            jax.ShapeDtypeStruct((pixels, count), BF16),
+            jax.ShapeDtypeStruct((count, pixels), BF16),
+        ],
+        scratch_shapes=[pltpu.VMEM((count, pixels), BF16), pltpu.SemaphoreType.DMA((2,))],
         compiler_params=pltpu.CompilerParams(vmem_limit_bytes=24 * 2**20),
         cost_estimate=pl.CostEstimate(
-            flops=3 * pixels * count, bytes_accessed=2 * pixels * count, transcendentals=0
+            flops=6 * pixels * count, bytes_accessed=4 * pixels * count, transcendentals=0
         ),
         name="tables",
-    )(cat, sat, cbt, sbt)
-    return (ca, sa), (cb, sb), flipped
+    )(ca, sa, cb, sb, cat, sat, cbt, sbt)
 
 
 def rotation(order_table, pixels):
@@ -166,12 +188,11 @@
 
 
 def cell_kernel(
-    in_ref, ca_ref, sa_ref, cb_ref, sb_ref, analysis_ref, turn_ref, parity_ref, out_ref, products, synth, analysis, sem, *, block
+    in_ref, synth_ref, analysis_ref, turn_ref, parity_ref, out_ref, products, analysis, sem, *, block
 ):
     count, pixels = analysis_ref.shape
     fetch_analysis = pltpu.make_async_copy(analysis_ref, analysis, sem)
     fetch_analysis.start()
-    low = cb_ref.shape[0]
     groups = in_ref.shape[1]
     step = products.shape[1] // (2 * LANES)
     width = step * LANES
@@ -195,12 +216,7 @@
                 turned[f].append((rot_cos * x + rot_sin * swap(x)).astype(BF16))
         turned = jnp.concatenate(turned[0] + turned[1], 1)
         for j in range(0, pixels, block):
-            if first == 0:
-                for a in range(j // low, (j + block) // low):
-                    synth[a * low : (a + 1) * low, :] = (
-                        ca_ref[a : a + 1, :] * cb_ref[...] - sa_ref[a : a + 1, :] * sb_ref[...]
-                    ).astype(BF16)
-            fields = jnp.dot(synth[j : j + block, :], turned, preferred_element_type=F32)
+            fields = jnp.dot(synth_ref[j : j + block, :], turned, preferred_element_type=F32)
             alpha, beta = fields[:, :width], fields[:, width:]
             products[j : j + block, :width] = (beta * beta).astype(BF16)
             products[j : j + block, width:] = (alpha * beta).astype(BF16)
@@ -216,30 +232,29 @@
             out_ref[first + g] = jnp.concatenate(parts, 1).astype(BF16)
 
 
-def cells(arrived, high, low, analysis, turn, parity, step=4, block=1024):
+def cells(arrived, synth, analysis, turn, parity, step=4, block=1024):
     owners, groups, rows, lanes = arrived.shape
     count, pixels = analysis.shape
     whole = pl.BlockSpec(memory_space=pltpu.VMEM)
     anywhere = pl.BlockSpec(memory_space=pltpu.HBM)
     return pl.pallas_call(
         functools.partial(cell_kernel, block=block),
-        in_specs=[*[whole] * 5, anywhere, whole, whole],
+        in_specs=[whole, whole, anywhere, whole, whole],
         out_specs=whole,
         out_shape=jax.ShapeDtypeStruct((groups, owners, rows, lanes), BF16),
         scratch_shapes=[
             pltpu.VMEM((pixels, 2 * step * lanes), BF16),
-            pltpu.VMEM((pixels, count), BF16),
             pltpu.VMEM((count, pixels), BF16),
             pltpu.SemaphoreType.DMA,
         ],
-        compiler_params=pltpu.CompilerParams(vmem_limit_bytes=50 * 2**20),
+        compiler_params=pltpu.CompilerParams(vmem_limit_bytes=48 * 2**20),
         cost_estimate=pl.CostEstimate(
             flops=2 * 2 * pixels * count * groups * 2 * lanes,
             bytes_accessed=4 * pixels * count + 2**22,
             transcendentals=0,
         ),
         name="cells",
-    )(arrived, *high, *low, analysis, turn, parity)
+    )(arrived, synth, analysis, turn, parity)
 
 
 def backward_kernel(
@@ -363,12 +378,12 @@
     arrived = lax.all_to_all(outgoing, "sht", 0, 0, tiled=True)
     parity = jnp.tile(((cycle_table - NSIDE + 1) % 2).astype(F32), 8)[None]
     turn = rotation(order_table, pixels)
-    high, low, analysis = tables(order_table, pixels)
+    synth, analysis = tables(order_table, pixels)
     radial, analysis = lax.optimization_barrier((radial, analysis))
     profile = radial * node_weight[:, None, None] * jnp.array([2.0, 4.0], F32)[None, :, None]
     near = jnp.stack([profile] + [swapped(profile, bit) for bit in (1, 2, 3)])
     far = swapped(near, 4)
-    returning = cells(arrived, high, low, analysis, turn, parity)
+    returning = cells(arrived, synth, analysis, turn, parity)
     returning, far = lax.optimization_barrier((returning, far))
     returning = returning.reshape(groups * owners, 16, LANES)
     at_orders = lax.all_to_all(returning, ("node", "sht"), 0, 0, tiled=True)

time: 109 us -> 108 us (level)
    all_to_all x1, waiting for transfers between devices: 15.5 us -> 14.2 us  [on_device(): arrived = lax.all_to_all(outgoing, 'sht', 0, 0, tiled=True)]
  transfers between devices with their start and end apart: 6 -> 6, of which waited for: 4 -> 5; matrix products, arithmetic and copies ran while one was open for 3% -> 3% of each run, Pallas kernels for 13% -> 13%
where the time goes in v5:
time: 108 us
  waiting for transfers between devices  49.2 us (46%)
  Pallas kernels  28.1 us (26%)
  starting transfers between devices  25.4 us (24%)
  other arithmetic  2.24 us (2%)
  local copies, waits for them, and re-layouts  2.23 us (2%)
    all_to_all x1, waiting for transfers between devices, on_device(): at_orders = lax.all_to_all(returning, ('node', 'sht'), 0, 0, tiled=True)  32 us
    all_to_all x1, waiting for transfers between devices, on_device(): arrived = lax.all_to_all(outgoing, 'sht', 0, 0, tiled=True)  14.2 us
    all_to_all x1, starting transfers between devices, on_device(): arrived = lax.all_to_all(outgoing, 'sht', 0, 0, tiled=True)  12.9 us
    pallas_call x1, Pallas kernels, cells(): pl.pallas_call(functools.partial(cell_kernel, block=block), in_specs=[who...  10.5 us
    pallas_call x1, Pallas kernels, forward(): pl.pallas_call(forward_kernel, grid=(orders_dev,), in_specs=[pl.BlockSpec...  7.88 us
    all_to_all x1, starting transfers between devices, on_device(): at_orders = lax.all_to_all(returning, ('node', 'sht'), 0, 0, tiled=True)  7.8 us
    pallas_call x1, Pallas kernels, backward(): pl.pallas_call(backward_kernel, grid_spec=pltpu.PrefetchScalarGridSpec(nu...  6.64 us
    ppermute x4, starting transfers between devices, swapped(): lax.ppermute(value, 'node', [(i, i ^ bit) for i in range(lax.axis_size('n...  4.71 us
  transfers between devices with their start and end apart: 6, of which 5 were waited for; matrix products, arithmetic and copies ran while one was open for 3% of the time, Pallas kernels for 13%

profile of v5, /device:TPU:1, one launch (start us, length us, event | category | flops | bytes accessed | tf_op | source)
XLA Modules:
  0.0 107.5 jit_solution(18293364798367606296)
XLA Ops:
  0.0 7.9 %forward.1 = bf16[32,8,16,128]{3,2,1,0:T(8,128)(2,1)} custom-call(bf16[4,32,2,2048]{3,2,1,0:T(2,128)(2,1)} %harm_ref.1, f32[2,2,2048]{2,1,0:T(2,128)} %radial_ref.1, bf16[4,2048,512]{2,1,0:T(8,128)(2,1)} %leg_ref.3), custom_call_target="tpu_custom_call" | custom-call | flops 2147483648 | bytes 10485760 | tf_op jit(solution)/shard_map/forward/pallas_call | solution.py:89
  7.9 0.0 copy-start.4
  7.9 0.0 copy-start.1
  7.9 0.0 copy-start.2
  7.9 0.0 copy-start.3
  7.9 0.0 copy-start.5
  7.9 12.9 %all-to-all-start = ((bf16[32,8,16,128]{3,2,1,0:T(8,128)(2,1)}), bf16[32,8,16,128]{3,2,1,0:T(8,128)(2,1)S(1)}, u32[]{:S(2)}, u32[]{:S(2)}) async-start(bf16[32,8,16,128]{3,2,1,0:T(8,128)(2,1)} %forward.1), calls=%async_computation | async-start | bytes 2097152 | tf_op jit(solution)/shard_map/all_to_all | solution.py:378
  20.9 0.1 mul.218
  21.0 0.0 copy-done.4
  21.0 0.1 broadcast_in_dim.12
  21.1 0.1 mul.210
  21.2 0.1 fusion.13
  21.3 0.1 copy.15
  21.4 0.5 multiply_sine_fusion
  21.9 0.5 fusion.11
  22.4 0.6 fusion.3
  23.1 3.1 %tables.1 = (bf16[4096,256]{1,0:T(8,128)(2,1)S(1)}, bf16[256,4096]{1,0:T(8,128)(2,1)S(1)}) custom-call(f32[64,256]{1,0:T(8,128)S(1)} %get-tuple-element.43.ca_ref, f32[64,256]{1,0:T(8,128)S(1)} %get-tuple-element.44.sa_ref, f32[64,256]{1,0:T(8,128)S(1)} %get-tuple-element.36.cb_ref, f32[64,256]{1,0:T(8,128)S(1)} %get-tuple-element.35.sb_ref, ...), custom_call_target="tpu_custom_call" | custom-call | flops 6291456 | bytes 4194304 | tf_op jit(solution)/shard_map/tables/pallas_call | solution.py:164
  26.1 0.0 copy-start
  26.1 1.3 %copy-done = bf16[256,4096]{1,0:T(8,128)(2,1)} copy-done((bf16[256,4096]{1,0:T(8,128)(2,1)}, bf16[256,4096]{1,0:T(8,128)(2,1)S(1)}, u32[]{:S(2)}) %copy-start) | copy-done | bytes 2097176
  27.5 0.0 copy-done.1
  27.5 0.0 copy-done.2
  27.5 0.0 copy-done.3
  27.5 0.1 multiply_multiply_fusion
  27.6 2.8 %collective-permute-start.1 = (f32[2,2,2048]{2,1,0:T(2,128)S(1)}, f32[2,2,2048]{2,1,0:T(2,128)S(1)}, u32[]{:S(2)}, u32[]{:S(2)}) collective-permute-start(f32[2,2,2048]{2,1,0:T(2,128)S(1)} %multiply_multiply_fusion), channel_id=1, source_target_pairs={{0,64},{32,96},{64,0},{96,32},{128,192},{160,224},{192,128},{224,1... | collective-permute-start | bytes 98312 | tf_op jit(solution)/shard_map/ppermute | solution.py:367
  30.4 0.3 collective-permute-start
  30.7 0.6 collective-permute-start.2
  31.3 0.1 reshape.204
  31.4 0.1 convert_element_type.70
  31.5 0.0 copy-done.5
  31.5 0.1 fusion.25
  31.6 0.1 sine_multiply_fusion.1
  31.7 0.1 fusion.29
  31.8 0.1 broadcast_in_dim_tile.3.parity_ref
  31.9 0.1 copy.16.turn_ref
  32.0 0.2 collective-permute-done.1
  32.2 1.2 %collective-permute-done = f32[2,2,2048]{2,1,0:T(2,128)S(1)} collective-permute-done((f32[2,2,2048]{2,1,0:T(2,128)S(1)}, f32[2,2,2048]{2,1,0:T(2,128)S(1)}, u32[]{:S(2)}, u32[]{:S(2)}) %collective-permute-start) | collective-permute-done | bytes 32800 | tf_op jit(solution)/shard_map/ppermute | solution.py:367
  33.5 1.5 %collective-permute-done.2 = f32[2,2,2048]{2,1,0:T(2,128)S(1)} collective-permute-done((f32[2,2,2048]{2,1,0:T(2,128)S(1)}, f32[2,2,2048]{2,1,0:T(2,128)S(1)}, u32[]{:S(2)}, u32[]{:S(2)}) %collective-permute-start.2) | collective-permute-done | bytes 32800 | tf_op jit(solution)/shard_map/ppermute | solution.py:367
  35.0 0.1 pad_maximum_fusion.near_ref
  35.1 1.0 collective-permute-start.3
  36.1 14.2 %all-to-all-done.in_ref = bf16[32,8,16,128]{3,2,1,0:T(8,128)(2,1)S(1)} async-done(((bf16[32,8,16,128]{3,2,1,0:T(8,128)(2,1)}), bf16[32,8,16,128]{3,2,1,0:T(8,128)(2,1)S(1)}, u32[]{:S(2)}, u32[]{:S(2)}) %all-to-all-start) | async-done | bytes 1048608 | tf_op jit(solution)/shard_map/all_to_all | solution.py:378
  50.2 10.5 %cells.1 = bf16[8,32,16,128]{3,2,1,0:T(8,128)(2,1)} custom-call(bf16[32,8,16,128]{3,2,1,0:T(8,128)(2,1)S(1)} %all-to-all-done.in_ref, bf16[4096,256]{1,0:T(8,128)(2,1)S(1)} %get-tuple-element.18.synth_ref, bf16[256,4096]{1,0:T(8,128)(2,1)} %copy-done, f32[256,4]{1,0:T(8,128)S(1)} %copy.16.turn_ref, f32[1,128]{1,0:T(1,128)S(1)} %broadcast_in_dim_tile.3.parity_ref), custom_call_target="tpu_custom_call" | custom-call | flops 8589934592 | bytes 8388608 | tf_op jit(solution)/shard_map/cells/pallas_call | solution.py:240
  60.8 0.0 collective-permute-done.3.far_ref
  60.8 7.8 %all-to-all-start.1 = ((bf16[256,16,128]{2,1,0:T(8,128)(2,1)}), bf16[256,16,128]{2,1,0:T(8,128)(2,1)S(1)}, u32[]{:S(2)}, u32[]{:S(2)}) async-start(bf16[256,16,128]{2,1,0:T(8,128)(2,1)} %bitcast.6), calls=%async_computation.1 | async-start | bytes 2097152 | tf_op jit(solution)/shard_map/all_to_all | solution.py:389
  68.6 0.1 pad_add_fusion.place_ref
  68.7 32.0 %all-to-all-done.1 = bf16[256,16,128]{2,1,0:T(8,128)(2,1)S(1)} async-done(((bf16[256,16,128]{2,1,0:T(8,128)(2,1)}), bf16[256,16,128]{2,1,0:T(8,128)(2,1)S(1)}, u32[]{:S(2)}, u32[]{:S(2)}) %all-to-all-start.1) | async-done | bytes 1048608 | tf_op jit(solution)/shard_map/all_to_all | solution.py:389
  100.7 6.6 %backward.1 = f32[4,4,2,2048]{3,2,1,0:T(2,128)} custom-call(s32[2]{0:T(128)S(1)} %pad_add_fusion.place_ref, bf16[8,32,16,128]{3,2,1,0:T(8,128)(2,1)S(1)} %bitcast.9, f32[4,2,2,2048]{3,2,1,0:T(2,128)S(1)} %pad_maximum_fusion.near_ref, f32[4,2,2,2048]{3,2,1,0:T(2,128)S(1)} %collective-permute-done.3.far_ref, bf16[4,2048,512]{2,1,0:T(8,128)(2,1)} %leg_ref.3), custom_call_target="tpu_custom_call" | custom-call | flops 2147483648 | bytes 10485760 | tf_op jit(solution)/shard_map/backward/pallas_call | solution.py:335
  (8 shorter events, 0.1 us)
Async XLA Ops:
  7.9 13.1 %copy-start.4 = (s32[128]{0:T(128)S(1)}, s32[128]{0:T(128)}, u32[]{:S(2)}) copy-start(s32[128]{0:T(128)} %param.11) | copy-start | bytes 1540
  7.9 19.6 %copy-start.1 = (f32[2,2,2048]{2,1,0:T(2,128)S(1)}, f32[2,2,2048]{2,1,0:T(2,128)}, u32[]{:S(2)}) copy-start(f32[2,2,2048]{2,1,0:T(2,128)} %radial_ref.1) | copy-start | bytes 98308
  7.9 19.6 %copy-start.2 = (f32[2]{0:T(128)S(1)}, f32[2]{0:T(128)}, u32[]{:S(2)}) copy-start(f32[2]{0:T(128)} %param.9) | copy-start | bytes 28
  7.9 19.6 %copy-start.3 = (f32[2]{0:T(128)S(1)}, f32[2]{0:T(128)}, u32[]{:S(2)}) copy-start(f32[2]{0:T(128)} %constant.120.clone) | copy-start | bytes 28
  7.9 23.6 %copy-start.5 = (s32[16]{0:T(128)S(1)}, s32[16]{0:T(128)}, u32[]{:S(2)}) copy-start(s32[16]{0:T(128)} %param.12) | copy-start | bytes 196
  7.9 42.3 %all-to-all-start = ((bf16[32,8,16,128]{3,2,1,0:T(8,128)(2,1)}), bf16[32,8,16,128]{3,2,1,0:T(8,128)(2,1)S(1)}, u32[]{:S(2)}, u32[]{:S(2)}) async-start(bf16[32,8,16,128]{3,2,1,0:T(8,128)(2,1)} %forward.1), calls=%async_computation | async-start | bytes 2097152 | tf_op jit(solution)/shard_map/all_to_all | solution.py:378
  26.1 1.3 %copy-start = (bf16[256,4096]{1,0:T(8,128)(2,1)}, bf16[256,4096]{1,0:T(8,128)(2,1)S(1)}, u32[]{:S(2)}) copy-start(bf16[256,4096]{1,0:T(8,128)(2,1)S(1)} %get-tuple-element.21.analysis_ref) | copy-start | bytes 6291460
  27.6 4.7 %collective-permute-start.1 = (f32[2,2,2048]{2,1,0:T(2,128)S(1)}, f32[2,2,2048]{2,1,0:T(2,128)S(1)}, u32[]{:S(2)}, u32[]{:S(2)}) collective-permute-start(f32[2,2,2048]{2,1,0:T(2,128)S(1)} %multiply_multiply_fusion), channel_id=1, source_target_pairs={{0,64},{32,96},{64,0},{96,32},{128,192},{160,224},{192,128},{224,1... | collective-permute-start | bytes 98312 | tf_op jit(solution)/shard_map/ppermute | solution.py:367
  30.4 3.1 %collective-permute-start = (f32[2,2,2048]{2,1,0:T(2,128)S(1)}, f32[2,2,2048]{2,1,0:T(2,128)S(1)}, u32[]{:S(2)}, u32[]{:S(2)}) collective-permute-start(f32[2,2,2048]{2,1,0:T(2,128)S(1)} %multiply_multiply_fusion), channel_id=1, source_target_pairs={{0,32},{32,0},{64,96},{96,64},{128,160},{160,128},{192,224},{224,1... | collective-permute-start | bytes 98312 | tf_op jit(solution)/shard_map/ppermute | solution.py:367
  30.7 4.3 %collective-permute-start.2 = (f32[2,2,2048]{2,1,0:T(2,128)S(1)}, f32[2,2,2048]{2,1,0:T(2,128)S(1)}, u32[]{:S(2)}, u32[]{:S(2)}) collective-permute-start(f32[2,2,2048]{2,1,0:T(2,128)S(1)} %multiply_multiply_fusion), channel_id=1, source_target_pairs={{0,96},{32,64},{64,32},{96,0},{128,224},{160,192},{192,160},{224,1... | collective-permute-start | bytes 98312 | tf_op jit(solution)/shard_map/ppermute | solution.py:367
  35.1 25.7 %collective-permute-start.3 = (f32[4,2,2,2048]{3,2,1,0:T(2,128)S(1)}, f32[4,2,2,2048]{3,2,1,0:T(2,128)S(1)}, u32[]{:S(2)}, u32[]{:S(2)}) collective-permute-start(f32[4,2,2,2048]{3,2,1,0:T(2,128)S(1)} %pad_maximum_fusion.near_ref), channel_id=1, source_target_pairs={{0,128},{32,160},{64,192},{96,224},{128,0},{160,32},{192,64},{224,... | collective-permute-start | bytes 393224 | tf_op jit(solution)/shard_map/ppermute | solution.py:367
  60.8 39.9 %all-to-all-start.1 = ((bf16[256,16,128]{2,1,0:T(8,128)(2,1)}), bf16[256,16,128]{2,1,0:T(8,128)(2,1)S(1)}, u32[]{:S(2)}, u32[]{:S(2)}) async-start(bf16[256,16,128]{2,1,0:T(8,128)(2,1)} %bitcast.6), calls=%async_computation.1 | async-start | bytes 2097152 | tf_op jit(solution)/shard_map/all_to_all | solution.py:389

commit v6 on v5

--- a/solution.py
+++ b/solution.py
@@ -27,7 +27,7 @@
     return value if count == 0 else pltpu.roll(value, 16 * count, 1)
 
 
-def forward_kernel(harm_ref, radial_ref, leg_ref, out_ref, lines, staged):
+def forward_kernel(harm_ref, radial_ref, leg_ref, out_ref, lines, staged, done, sems):
     order = pl.program_id(0)
     samples, degrees = harm_ref.shape[1], harm_ref.shape[3]
     nodes = radial_ref.shape[0]
@@ -73,12 +73,18 @@
     @pl.when(order == 3)
     def _():
         size = groups * 16
+        copies = []
         for lane in range(staged.shape[0]):
             blocks = deal_blocks(
                 [shift_blocks(staged[lane, i * size : (i + 1) * size, :], i) for i in range(8)]
             )
             for i in range(8):
-                out_ref[lane * 8 + i] = blocks[i].astype(BF16).reshape(groups, 16, LANES)
+                done[lane * 8 + i] = blocks[i].astype(BF16).reshape(groups, 16, LANES)
+            piece = pl.ds(lane * 8, 8)
+            copies.append(pltpu.make_async_copy(done.at[piece], out_ref.at[piece], sems.at[lane]))
+            copies[-1].start()
+        for copy in copies:
+            copy.wait()
 
 
 def forward(harmonics, radial, legendre):
@@ -94,10 +100,12 @@
             pl.BlockSpec(radial.shape, lambda o: (0, 0, 0)),
             pl.BlockSpec((1, degrees, cycles), lambda o: (o, 0, 0)),
         ],
-        out_specs=pl.BlockSpec(out, lambda o: (0, 0, 0, 0)),
+        out_specs=pl.BlockSpec(memory_space=pltpu.HBM),
         scratch_shapes=[
             pltpu.VMEM((degrees // LANES, samples * 2, LANES), F32),
             pltpu.VMEM((cycles // LANES, nodes * samples * 16, LANES), F32),
+            pltpu.VMEM(out, BF16),
+            pltpu.SemaphoreType.DMA((cycles // LANES,)),
         ],
         out_shape=jax.ShapeDtypeStruct(out, BF16),
         compiler_params=pltpu.CompilerParams(vmem_limit_bytes=58 * 2**20),
@@ -229,7 +237,7 @@
                 at = p * width + g * LANES
                 x = spectra[:, at : at + LANES]
                 parts.append((back_cos * x - back_sin * swap(x)).reshape(count // 8, 8, LANES))
-            out_ref[first + g] = jnp.concatenate(parts, 1).astype(BF16)
+            out_ref[:, first + g] = jnp.concatenate(parts, 1).astype(BF16)
 
 
 def cells(arrived, synth, analysis, turn, parity, step=4, block=1024):
@@ -241,7 +249,7 @@
         functools.partial(cell_kernel, block=block),
         in_specs=[whole, whole, anywhere, whole, whole],
         out_specs=whole,
-        out_shape=jax.ShapeDtypeStruct((groups, owners, rows, lanes), BF16),
+        out_shape=jax.ShapeDtypeStruct((owners, groups, rows, lanes), BF16),
         scratch_shapes=[
             pltpu.VMEM((pixels, 2 * step * lanes), BF16),
             pltpu.VMEM((count, pixels), BF16),
@@ -262,7 +270,7 @@
 ):
     step = pl.program_id(0)
     orders_dev, degrees = leg_ref.shape[:2]
-    sources, cells_in = in_ref.shape[:2]
+    cells_in, sources = in_ref.shape[:2]
     chunks = staged.shape[0]
     per = cells_in // chunks
     rows = sources * per
@@ -278,7 +286,7 @@
         def chunk(lane, carry):
             blocks = deal_blocks(
                 [
-                    in_ref[:, lane * per + i].astype(F32).reshape(sources * 16, LANES)
+                    in_ref[lane * per + i].astype(F32).reshape(sources * 16, LANES)
                     for i in range(per)
                 ]
             )
@@ -329,7 +337,7 @@
 
 
 def backward(place, at_orders, profiles, legendre):
-    sources = at_orders.shape[0]
+    sources = at_orders.shape[1]
     orders_dev, degrees, cycles = legendre.shape
     near = profiles[0].shape
     return pl.pallas_call(
@@ -385,9 +393,9 @@
     far = swapped(near, 4)
     returning = cells(arrived, synth, analysis, turn, parity)
     returning, far = lax.optimization_barrier((returning, far))
-    returning = returning.reshape(groups * owners, 16, LANES)
-    at_orders = lax.all_to_all(returning, ("node", "sht"), 0, 0, tiled=True)
-    at_orders = at_orders.reshape(groups, owners, 16, LANES)
+    returning = returning.reshape(owners * groups, 16, LANES)
+    at_orders = lax.all_to_all(returning, ("sht", "node"), 0, 0, tiled=True)
+    at_orders = at_orders.reshape(owners, groups, 16, LANES)
     node = lax.axis_index("node").astype(jnp.int32)
     place = jnp.stack([node // 4, node % 4])
     return backward(place, at_orders, (near, far), legendre)

time: 108 us -> 108 us (level)
  no operation moved by 1% of the time
where the time goes in v6:
time: 108 us; the launch traced here: 107 us
  waiting for transfers between devices  49.2 us (46%)
  Pallas kernels  27.9 us (26%)
  starting transfers between devices  25.5 us (24%)
  local copies, waits for them, and re-layouts  2.24 us (2%)
  other arithmetic  2.24 us (2%)
    all_to_all x1, waiting for transfers between devices, on_device(): at_orders = lax.all_to_all(returning, ('sht', 'node'), 0, 0, tiled=True)  32.1 us
    all_to_all x1, waiting for transfers between devices, on_device(): arrived = lax.all_to_all(outgoing, 'sht', 0, 0, tiled=True)  14.1 us
    all_to_all x1, starting transfers between devices, on_device(): arrived = lax.all_to_all(outgoing, 'sht', 0, 0, tiled=True)  12.9 us
    pallas_call x1, Pallas kernels, cells(): pl.pallas_call(functools.partial(cell_kernel, block=block), in_specs=[who...  10.5 us
    all_to_all x1, starting transfers between devices, on_device(): at_orders = lax.all_to_all(returning, ('sht', 'node'), 0, 0, tiled=True)  7.92 us
    pallas_call x1, Pallas kernels, forward(): pl.pallas_call(forward_kernel, grid=(orders_dev,), in_specs=[pl.BlockSpec...  7.64 us
    pallas_call x1, Pallas kernels, backward(): pl.pallas_call(backward_kernel, grid_spec=pltpu.PrefetchScalarGridSpec(nu...  6.64 us
    ppermute x4, starting transfers between devices, swapped(): lax.ppermute(value, 'node', [(i, i ^ bit) for i in range(lax.axis_size('n...  4.71 us
  transfers between devices with their start and end apart: 6, of which 5 were waited for; matrix products, arithmetic and copies ran while one was open for 3% of the time, Pallas kernels for 13%

profile of v6, /device:TPU:1, one launch (start us, length us, event | category | flops | bytes accessed | tf_op | source)
XLA Modules:
  0.0 107.4 jit_solution(14128914103362459595)
XLA Ops:
  0.0 7.6 %forward.1 = bf16[32,8,16,128]{3,2,1,0:T(8,128)(2,1)} custom-call(bf16[4,32,2,2048]{3,2,1,0:T(2,128)(2,1)} %harm_ref.1, f32[2,2,2048]{2,1,0:T(2,128)} %radial_ref.1, bf16[4,2048,512]{2,1,0:T(8,128)(2,1)} %leg_ref.3), custom_call_target="tpu_custom_call" | custom-call | flops 2147483648 | bytes 10485760 | tf_op jit(solution)/shard_map/forward/pallas_call | solution.py:95
  7.7 0.0 copy-start.4
  7.7 0.0 copy-start.1
  7.7 0.0 copy-start.2
  7.7 0.0 copy-start.3
  7.7 0.0 copy-start.5
  7.7 12.9 %all-to-all-start = ((bf16[32,8,16,128]{3,2,1,0:T(8,128)(2,1)}), bf16[32,8,16,128]{3,2,1,0:T(8,128)(2,1)S(1)}, u32[]{:S(2)}, u32[]{:S(2)}) async-start(bf16[32,8,16,128]{3,2,1,0:T(8,128)(2,1)} %forward.1), calls=%async_computation | async-start | bytes 2097152 | tf_op jit(solution)/shard_map/all_to_all | solution.py:386
  20.7 0.1 mul.218
  20.8 0.0 copy-done.4
  20.8 0.1 broadcast_in_dim.12
  20.9 0.1 mul.210
  21.0 0.1 fusion.13
  21.1 0.1 copy.15
  21.2 0.5 multiply_sine_fusion
  21.7 0.5 fusion.11
  22.2 0.6 fusion.3
  22.9 3.1 %tables.1 = (bf16[4096,256]{1,0:T(8,128)(2,1)S(1)}, bf16[256,4096]{1,0:T(8,128)(2,1)S(1)}) custom-call(f32[64,256]{1,0:T(8,128)S(1)} %get-tuple-element.43.ca_ref, f32[64,256]{1,0:T(8,128)S(1)} %get-tuple-element.44.sa_ref, f32[64,256]{1,0:T(8,128)S(1)} %get-tuple-element.36.cb_ref, f32[64,256]{1,0:T(8,128)S(1)} %get-tuple-element.35.sb_ref, ...), custom_call_target="tpu_custom_call" | custom-call | flops 6291456 | bytes 4194304 | tf_op jit(solution)/shard_map/tables/pallas_call | solution.py:172
  25.9 0.0 copy-start
  25.9 1.3 %copy-done = bf16[256,4096]{1,0:T(8,128)(2,1)} copy-done((bf16[256,4096]{1,0:T(8,128)(2,1)}, bf16[256,4096]{1,0:T(8,128)(2,1)S(1)}, u32[]{:S(2)}) %copy-start) | copy-done | bytes 2097176
  27.3 0.0 copy-done.1
  27.3 0.0 copy-done.2
  27.3 0.0 copy-done.3
  27.3 0.1 multiply_multiply_fusion
  27.4 2.8 %collective-permute-start.1 = (f32[2,2,2048]{2,1,0:T(2,128)S(1)}, f32[2,2,2048]{2,1,0:T(2,128)S(1)}, u32[]{:S(2)}, u32[]{:S(2)}) collective-permute-start(f32[2,2,2048]{2,1,0:T(2,128)S(1)} %multiply_multiply_fusion), channel_id=1, source_target_pairs={{0,64},{32,96},{64,0},{96,32},{128,192},{160,224},{192,128},{224,1... | collective-permute-start | bytes 98312 | tf_op jit(solution)/shard_map/ppermute | solution.py:375
  30.2 0.3 collective-permute-start
  30.5 0.6 collective-permute-start.2
  31.1 0.1 reshape.204
  31.2 0.1 convert_element_type.70
  31.3 0.0 copy-done.5
  31.3 0.1 fusion.25
  31.4 0.1 sine_multiply_fusion.1
  31.5 0.1 fusion.29
  31.6 0.1 broadcast_in_dim_tile.3.parity_ref
  31.7 0.1 copy.16.turn_ref
  31.8 0.2 collective-permute-done.1
  32.0 1.2 %collective-permute-done = f32[2,2,2048]{2,1,0:T(2,128)S(1)} collective-permute-done((f32[2,2,2048]{2,1,0:T(2,128)S(1)}, f32[2,2,2048]{2,1,0:T(2,128)S(1)}, u32[]{:S(2)}, u32[]{:S(2)}) %collective-permute-start) | collective-permute-done | bytes 32800 | tf_op jit(solution)/shard_map/ppermute | solution.py:375
  33.3 1.5 %collective-permute-done.2 = f32[2,2,2048]{2,1,0:T(2,128)S(1)} collective-permute-done((f32[2,2,2048]{2,1,0:T(2,128)S(1)}, f32[2,2,2048]{2,1,0:T(2,128)S(1)}, u32[]{:S(2)}, u32[]{:S(2)}) %collective-permute-start.2) | collective-permute-done | bytes 32800 | tf_op jit(solution)/shard_map/ppermute | solution.py:375
  34.8 0.1 pad_maximum_fusion.near_ref
  34.9 1.0 collective-permute-start.3
  35.9 14.1 %all-to-all-done.in_ref = bf16[32,8,16,128]{3,2,1,0:T(8,128)(2,1)S(1)} async-done(((bf16[32,8,16,128]{3,2,1,0:T(8,128)(2,1)}), bf16[32,8,16,128]{3,2,1,0:T(8,128)(2,1)S(1)}, u32[]{:S(2)}, u32[]{:S(2)}) %all-to-all-start) | async-done | bytes 1048608 | tf_op jit(solution)/shard_map/all_to_all | solution.py:386
  50.0 10.5 %cells.1 = bf16[32,8,16,128]{3,2,1,0:T(8,128)(2,1)} custom-call(bf16[32,8,16,128]{3,2,1,0:T(8,128)(2,1)S(1)} %all-to-all-done.in_ref, bf16[4096,256]{1,0:T(8,128)(2,1)S(1)} %get-tuple-element.18.synth_ref, bf16[256,4096]{1,0:T(8,128)(2,1)} %copy-done, f32[256,4]{1,0:T(8,128)S(1)} %copy.16.turn_ref, f32[1,128]{1,0:T(1,128)S(1)} %broadcast_in_dim_tile.3.parity_ref), custom_call_target="tpu_custom_call" | custom-call | flops 8589934592 | bytes 8388608 | tf_op jit(solution)/shard_map/cells/pallas_call | solution.py:248
  60.5 0.0 collective-permute-done.3.far_ref
  60.5 7.9 %all-to-all-start.1 = ((bf16[256,16,128]{2,1,0:T(8,128)(2,1)}), bf16[256,16,128]{2,1,0:T(8,128)(2,1)S(1)}, u32[]{:S(2)}, u32[]{:S(2)}) async-start(bf16[256,16,128]{2,1,0:T(8,128)(2,1)} %bitcast.6), calls=%async_computation.1 | async-start | bytes 2097152 | tf_op jit(solution)/shard_map/all_to_all | solution.py:397
  68.5 0.1 pad_add_fusion.place_ref
  68.5 32.1 %all-to-all-done.1 = bf16[256,16,128]{2,1,0:T(8,128)(2,1)S(1)} async-done(((bf16[256,16,128]{2,1,0:T(8,128)(2,1)}), bf16[256,16,128]{2,1,0:T(8,128)(2,1)S(1)}, u32[]{:S(2)}, u32[]{:S(2)}) %all-to-all-start.1) | async-done | bytes 1048608 | tf_op jit(solution)/shard_map/all_to_all | solution.py:397
  100.6 6.6 %backward.1 = f32[4,4,2,2048]{3,2,1,0:T(2,128)} custom-call(s32[2]{0:T(128)S(1)} %pad_add_fusion.place_ref, bf16[32,8,16,128]{3,2,1,0:T(8,128)(2,1)S(1)} %bitcast.9, f32[4,2,2,2048]{3,2,1,0:T(2,128)S(1)} %pad_maximum_fusion.near_ref, f32[4,2,2,2048]{3,2,1,0:T(2,128)S(1)} %collective-permute-done.3.far_ref, bf16[4,2048,512]{2,1,0:T(8,128)(2,1)} %leg_ref.3), custom_call_target="tpu_custom_call" | custom-call | flops 2147483648 | bytes 10485760 | tf_op jit(solution)/shard_map/backward/pallas_call | solution.py:343
  (8 shorter events, 0.1 us)
Async XLA Ops:
  7.7 13.1 %copy-start.4 = (s32[128]{0:T(128)S(1)}, s32[128]{0:T(128)}, u32[]{:S(2)}) copy-start(s32[128]{0:T(128)} %param.11) | copy-start | bytes 1540
  7.7 19.6 %copy-start.1 = (f32[2,2,2048]{2,1,0:T(2,128)S(1)}, f32[2,2,2048]{2,1,0:T(2,128)}, u32[]{:S(2)}) copy-start(f32[2,2,2048]{2,1,0:T(2,128)} %radial_ref.1) | copy-start | bytes 98308
  7.7 19.6 %copy-start.2 = (f32[2]{0:T(128)S(1)}, f32[2]{0:T(128)}, u32[]{:S(2)}) copy-start(f32[2]{0:T(128)} %param.9) | copy-start | bytes 28
  7.7 19.6 %copy-start.3 = (f32[2]{0:T(128)S(1)}, f32[2]{0:T(128)}, u32[]{:S(2)}) copy-start(f32[2]{0:T(128)} %constant.120.clone) | copy-start | bytes 28
  7.7 23.6 %copy-start.5 = (s32[16]{0:T(128)S(1)}, s32[16]{0:T(128)}, u32[]{:S(2)}) copy-start(s32[16]{0:T(128)} %param.12) | copy-start | bytes 196
  7.7 42.3 %all-to-all-start = ((bf16[32,8,16,128]{3,2,1,0:T(8,128)(2,1)}), bf16[32,8,16,128]{3,2,1,0:T(8,128)(2,1)S(1)}, u32[]{:S(2)}, u32[]{:S(2)}) async-start(bf16[32,8,16,128]{3,2,1,0:T(8,128)(2,1)} %forward.1), calls=%async_computation | async-start | bytes 2097152 | tf_op jit(solution)/shard_map/all_to_all | solution.py:386
  25.9 1.3 %copy-start = (bf16[256,4096]{1,0:T(8,128)(2,1)}, bf16[256,4096]{1,0:T(8,128)(2,1)S(1)}, u32[]{:S(2)}) copy-start(bf16[256,4096]{1,0:T(8,128)(2,1)S(1)} %get-tuple-element.21.analysis_ref) | copy-start | bytes 6291460
  27.4 4.7 %collective-permute-start.1 = (f32[2,2,2048]{2,1,0:T(2,128)S(1)}, f32[2,2,2048]{2,1,0:T(2,128)S(1)}, u32[]{:S(2)}, u32[]{:S(2)}) collective-permute-start(f32[2,2,2048]{2,1,0:T(2,128)S(1)} %multiply_multiply_fusion), channel_id=1, source_target_pairs={{0,64},{32,96},{64,0},{96,32},{128,192},{160,224},{192,128},{224,1... | collective-permute-start | bytes 98312 | tf_op jit(solution)/shard_map/ppermute | solution.py:375
  30.2 3.1 %collective-permute-start = (f32[2,2,2048]{2,1,0:T(2,128)S(1)}, f32[2,2,2048]{2,1,0:T(2,128)S(1)}, u32[]{:S(2)}, u32[]{:S(2)}) collective-permute-start(f32[2,2,2048]{2,1,0:T(2,128)S(1)} %multiply_multiply_fusion), channel_id=1, source_target_pairs={{0,32},{32,0},{64,96},{96,64},{128,160},{160,128},{192,224},{224,1... | collective-permute-start | bytes 98312 | tf_op jit(solution)/shard_map/ppermute | solution.py:375
  30.5 4.3 %collective-permute-start.2 = (f32[2,2,2048]{2,1,0:T(2,128)S(1)}, f32[2,2,2048]{2,1,0:T(2,128)S(1)}, u32[]{:S(2)}, u32[]{:S(2)}) collective-permute-start(f32[2,2,2048]{2,1,0:T(2,128)S(1)} %multiply_multiply_fusion), channel_id=1, source_target_pairs={{0,96},{32,64},{64,32},{96,0},{128,224},{160,192},{192,160},{224,1... | collective-permute-start | bytes 98312 | tf_op jit(solution)/shard_map/ppermute | solution.py:375
  34.9 25.6 %collective-permute-start.3 = (f32[4,2,2,2048]{3,2,1,0:T(2,128)S(1)}, f32[4,2,2,2048]{3,2,1,0:T(2,128)S(1)}, u32[]{:S(2)}, u32[]{:S(2)}) collective-permute-start(f32[4,2,2,2048]{3,2,1,0:T(2,128)S(1)} %pad_maximum_fusion.near_ref), channel_id=1, source_target_pairs={{0,128},{32,160},{64,192},{96,224},{128,0},{160,32},{192,64},{224,... | collective-permute-start | bytes 393224 | tf_op jit(solution)/shard_map/ppermute | solution.py:375
  60.5 40.1 %all-to-all-start.1 = ((bf16[256,16,128]{2,1,0:T(8,128)(2,1)}), bf16[256,16,128]{2,1,0:T(8,128)(2,1)S(1)}, u32[]{:S(2)}, u32[]{:S(2)}) async-start(bf16[256,16,128]{2,1,0:T(8,128)(2,1)} %bitcast.6), calls=%async_computation.1 | async-start | bytes 2097152 | tf_op jit(solution)/shard_map/all_to_all | solution.py:397

commit v7 on v6

--- a/solution.py
+++ b/solution.py
@@ -196,7 +196,7 @@
 
 
 def cell_kernel(
-    in_ref, synth_ref, analysis_ref, turn_ref, parity_ref, out_ref, products, analysis, sem, *, block
+    in_ref, synth_ref, analysis_ref, turn_ref, parity_ref, out_ref, products, analysis, sem, done, out_sems, *, block
 ):
     count, pixels = analysis_ref.shape
     fetch_analysis = pltpu.make_async_copy(analysis_ref, analysis, sem)
@@ -215,6 +215,7 @@
     def swap(x):
         return pltpu.roll(x.reshape(count // 8, 8, LANES), 4, 1).reshape(count, LANES)
 
+    copies = []
     for first in range(0, groups, step):
         turned = [[], []]
         for g in range(first, first + step):
@@ -237,10 +238,19 @@
                 at = p * width + g * LANES
                 x = spectra[:, at : at + LANES]
                 parts.append((back_cos * x - back_sin * swap(x)).reshape(count // 8, 8, LANES))
-            out_ref[:, first + g] = jnp.concatenate(parts, 1).astype(BF16)
-
-
-def cells(arrived, synth, analysis, turn, parity, step=4, block=1024):
+            done[:, first + g] = jnp.concatenate(parts, 1).astype(BF16)
+        piece = pl.ds(first, step)
+        copies.append(
+            pltpu.make_async_copy(
+                done.at[:, piece], out_ref.at[:, piece], out_sems.at[first // step]
+            )
+        )
+        copies[-1].start()
+    for copy in copies:
+        copy.wait()
+
+
+def cells(arrived, synth, analysis, turn, parity, step=2, block=1024):
     owners, groups, rows, lanes = arrived.shape
     count, pixels = analysis.shape
     whole = pl.BlockSpec(memory_space=pltpu.VMEM)
@@ -248,12 +258,14 @@
     return pl.pallas_call(
         functools.partial(cell_kernel, block=block),
         in_specs=[whole, whole, anywhere, whole, whole],
-        out_specs=whole,
+        out_specs=anywhere,
         out_shape=jax.ShapeDtypeStruct((owners, groups, rows, lanes), BF16),
         scratch_shapes=[
             pltpu.VMEM((pixels, 2 * step * lanes), BF16),
             pltpu.VMEM((count, pixels), BF16),
             pltpu.SemaphoreType.DMA,
+            pltpu.VMEM(arrived.shape, BF16),
+            pltpu.SemaphoreType.DMA((groups // step,)),
         ],
         compiler_params=pltpu.CompilerParams(vmem_limit_bytes=48 * 2**20),
         cost_estimate=pl.CostEstimate(

time: 108 us -> 108 us (level)
  transfers between devices with their start and end apart: 6 -> 6, of which waited for: 5 -> 5; matrix products, arithmetic and copies ran while one was open for 3% -> 3% of each run, Pallas kernels for 13% -> 12%
where the time goes in v7:
time: 108 us; the launch traced here: 107 us
  waiting for transfers between devices  49.2 us (46%)
  Pallas kernels  27.7 us (26%)
  starting transfers between devices  25.5 us (24%)
  local copies, waits for them, and re-layouts  2.24 us (2%)
  other arithmetic  2.24 us (2%)
    all_to_all x1, waiting for transfers between devices, on_device(): at_orders = lax.all_to_all(returning, ('sht', 'node'), 0, 0, tiled=True)  32.1 us
    all_to_all x1, waiting for transfers between devices, on_device(): arrived = lax.all_to_all(outgoing, 'sht', 0, 0, tiled=True)  14.1 us
    all_to_all x1, starting transfers between devices, on_device(): arrived = lax.all_to_all(outgoing, 'sht', 0, 0, tiled=True)  12.9 us
    pallas_call x1, Pallas kernels, cells(): pl.pallas_call(functools.partial(cell_kernel, block=block), in_specs=[who...  10.3 us
    all_to_all x1, starting transfers between devices, on_device(): at_orders = lax.all_to_all(returning, ('sht', 'node'), 0, 0, tiled=True)  7.93 us
    pallas_call x1, Pallas kernels, forward(): pl.pallas_call(forward_kernel, grid=(orders_dev,), in_specs=[pl.BlockSpec...  7.64 us
    pallas_call x1, Pallas kernels, backward(): pl.pallas_call(backward_kernel, grid_spec=pltpu.PrefetchScalarGridSpec(nu...  6.64 us
    ppermute x4, starting transfers between devices, swapped(): lax.ppermute(value, 'node', [(i, i ^ bit) for i in range(lax.axis_size('n...  4.71 us
  transfers between devices with their start and end apart: 6, of which 5 were waited for; matrix products, arithmetic and copies ran while one was open for 3% of the time, Pallas kernels for 12%

profile of v7, /device:TPU:1, one launch (start us, length us, event | category | flops | bytes accessed | tf_op | source)
XLA Modules:
  0.0 107.3 jit_solution(13718610164105091630)
XLA Ops:
  0.0 7.6 %forward.1 = bf16[32,8,16,128]{3,2,1,0:T(8,128)(2,1)} custom-call(bf16[4,32,2,2048]{3,2,1,0:T(2,128)(2,1)} %harm_ref.1, f32[2,2,2048]{2,1,0:T(2,128)} %radial_ref.1, bf16[4,2048,512]{2,1,0:T(8,128)(2,1)} %leg_ref.3), custom_call_target="tpu_custom_call" | custom-call | flops 2147483648 | bytes 10485760 | tf_op jit(solution)/shard_map/forward/pallas_call | solution.py:95
  7.7 0.0 copy-start.4
  7.7 0.0 copy-start.1
  7.7 0.0 copy-start.2
  7.7 0.0 copy-start.3
  7.7 0.0 copy-start.5
  7.7 12.9 %all-to-all-start = ((bf16[32,8,16,128]{3,2,1,0:T(8,128)(2,1)}), bf16[32,8,16,128]{3,2,1,0:T(8,128)(2,1)S(1)}, u32[]{:S(2)}, u32[]{:S(2)}) async-start(bf16[32,8,16,128]{3,2,1,0:T(8,128)(2,1)} %forward.1), calls=%async_computation | async-start | bytes 2097152 | tf_op jit(solution)/shard_map/all_to_all | solution.py:398
  20.7 0.1 mul.218
  20.8 0.0 copy-done.4
  20.8 0.1 broadcast_in_dim.12
  20.9 0.1 mul.210
  21.0 0.1 fusion.13
  21.1 0.1 copy.15
  21.2 0.5 multiply_sine_fusion
  21.7 0.5 fusion.11
  22.2 0.6 fusion.3
  22.9 3.1 %tables.1 = (bf16[4096,256]{1,0:T(8,128)(2,1)S(1)}, bf16[256,4096]{1,0:T(8,128)(2,1)S(1)}) custom-call(f32[64,256]{1,0:T(8,128)S(1)} %get-tuple-element.43.ca_ref, f32[64,256]{1,0:T(8,128)S(1)} %get-tuple-element.44.sa_ref, f32[64,256]{1,0:T(8,128)S(1)} %get-tuple-element.36.cb_ref, f32[64,256]{1,0:T(8,128)S(1)} %get-tuple-element.35.sb_ref, ...), custom_call_target="tpu_custom_call" | custom-call | flops 6291456 | bytes 4194304 | tf_op jit(solution)/shard_map/tables/pallas_call | solution.py:172
  25.9 0.0 copy-start
  25.9 1.3 %copy-done = bf16[256,4096]{1,0:T(8,128)(2,1)} copy-done((bf16[256,4096]{1,0:T(8,128)(2,1)}, bf16[256,4096]{1,0:T(8,128)(2,1)S(1)}, u32[]{:S(2)}) %copy-start) | copy-done | bytes 2097176
  27.3 0.0 copy-done.1
  27.3 0.0 copy-done.2
  27.3 0.0 copy-done.3
  27.3 0.1 multiply_multiply_fusion
  27.4 2.8 %collective-permute-start.1 = (f32[2,2,2048]{2,1,0:T(2,128)S(1)}, f32[2,2,2048]{2,1,0:T(2,128)S(1)}, u32[]{:S(2)}, u32[]{:S(2)}) collective-permute-start(f32[2,2,2048]{2,1,0:T(2,128)S(1)} %multiply_multiply_fusion), channel_id=1, source_target_pairs={{0,64},{32,96},{64,0},{96,32},{128,192},{160,224},{192,128},{224,1... | collective-permute-start | bytes 98312 | tf_op jit(solution)/shard_map/ppermute | solution.py:387
  30.2 0.3 collective-permute-start
  30.5 0.6 collective-permute-start.2
  31.1 0.1 reshape.204
  31.2 0.1 convert_element_type.70
  31.3 0.0 copy-done.5
  31.3 0.1 fusion.25
  31.4 0.1 sine_multiply_fusion.1
  31.5 0.1 fusion.29
  31.6 0.1 broadcast_in_dim_tile.3.parity_ref
  31.7 0.1 copy.16.turn_ref
  31.8 0.2 collective-permute-done.1
  32.0 1.2 %collective-permute-done = f32[2,2,2048]{2,1,0:T(2,128)S(1)} collective-permute-done((f32[2,2,2048]{2,1,0:T(2,128)S(1)}, f32[2,2,2048]{2,1,0:T(2,128)S(1)}, u32[]{:S(2)}, u32[]{:S(2)}) %collective-permute-start) | collective-permute-done | bytes 32800 | tf_op jit(solution)/shard_map/ppermute | solution.py:387
  33.3 1.5 %collective-permute-done.2 = f32[2,2,2048]{2,1,0:T(2,128)S(1)} collective-permute-done((f32[2,2,2048]{2,1,0:T(2,128)S(1)}, f32[2,2,2048]{2,1,0:T(2,128)S(1)}, u32[]{:S(2)}, u32[]{:S(2)}) %collective-permute-start.2) | collective-permute-done | bytes 32800 | tf_op jit(solution)/shard_map/ppermute | solution.py:387
  34.8 0.1 pad_maximum_fusion.near_ref
  34.9 1.0 collective-permute-start.3
  35.9 14.1 %all-to-all-done.in_ref = bf16[32,8,16,128]{3,2,1,0:T(8,128)(2,1)S(1)} async-done(((bf16[32,8,16,128]{3,2,1,0:T(8,128)(2,1)}), bf16[32,8,16,128]{3,2,1,0:T(8,128)(2,1)S(1)}, u32[]{:S(2)}, u32[]{:S(2)}) %all-to-all-start) | async-done | bytes 1048608 | tf_op jit(solution)/shard_map/all_to_all | solution.py:398
  50.0 10.3 %cells.1 = bf16[32,8,16,128]{3,2,1,0:T(8,128)(2,1)} custom-call(bf16[32,8,16,128]{3,2,1,0:T(8,128)(2,1)S(1)} %all-to-all-done.in_ref, bf16[4096,256]{1,0:T(8,128)(2,1)S(1)} %get-tuple-element.18.synth_ref, bf16[256,4096]{1,0:T(8,128)(2,1)} %copy-done, f32[256,4]{1,0:T(8,128)S(1)} %copy.16.turn_ref, f32[1,128]{1,0:T(1,128)S(1)} %broadcast_in_dim_tile.3.parity_ref), custom_call_target="tpu_custom_call" | custom-call | flops 8589934592 | bytes 8388608 | tf_op jit(solution)/shard_map/cells/pallas_call | solution.py:258
  60.3 0.0 collective-permute-done.3.far_ref
  60.3 7.9 %all-to-all-start.1 = ((bf16[256,16,128]{2,1,0:T(8,128)(2,1)}), bf16[256,16,128]{2,1,0:T(8,128)(2,1)S(1)}, u32[]{:S(2)}, u32[]{:S(2)}) async-start(bf16[256,16,128]{2,1,0:T(8,128)(2,1)} %bitcast.6), calls=%async_computation.1 | async-start | bytes 2097152 | tf_op jit(solution)/shard_map/all_to_all | solution.py:409
  68.3 0.1 pad_add_fusion.place_ref
  68.3 32.1 %all-to-all-done.1 = bf16[256,16,128]{2,1,0:T(8,128)(2,1)S(1)} async-done(((bf16[256,16,128]{2,1,0:T(8,128)(2,1)}), bf16[256,16,128]{2,1,0:T(8,128)(2,1)S(1)}, u32[]{:S(2)}, u32[]{:S(2)}) %all-to-all-start.1) | async-done | bytes 1048608 | tf_op jit(solution)/shard_map/all_to_all | solution.py:409
  100.5 6.6 %backward.1 = f32[4,4,2,2048]{3,2,1,0:T(2,128)} custom-call(s32[2]{0:T(128)S(1)} %pad_add_fusion.place_ref, bf16[32,8,16,128]{3,2,1,0:T(8,128)(2,1)S(1)} %bitcast.9, f32[4,2,2,2048]{3,2,1,0:T(2,128)S(1)} %pad_maximum_fusion.near_ref, f32[4,2,2,2048]{3,2,1,0:T(2,128)S(1)} %collective-permute-done.3.far_ref, bf16[4,2048,512]{2,1,0:T(8,128)(2,1)} %leg_ref.3), custom_call_target="tpu_custom_call" | custom-call | flops 2147483648 | bytes 10485760 | tf_op jit(solution)/shard_map/backward/pallas_call | solution.py:355
  (8 shorter events, 0.1 us)
Async XLA Ops:
  7.7 13.1 %copy-start.4 = (s32[128]{0:T(128)S(1)}, s32[128]{0:T(128)}, u32[]{:S(2)}) copy-start(s32[128]{0:T(128)} %param.11) | copy-start | bytes 1540
  7.7 19.6 %copy-start.1 = (f32[2,2,2048]{2,1,0:T(2,128)S(1)}, f32[2,2,2048]{2,1,0:T(2,128)}, u32[]{:S(2)}) copy-start(f32[2,2,2048]{2,1,0:T(2,128)} %radial_ref.1) | copy-start | bytes 98308
  7.7 19.6 %copy-start.2 = (f32[2]{0:T(128)S(1)}, f32[2]{0:T(128)}, u32[]{:S(2)}) copy-start(f32[2]{0:T(128)} %param.9) | copy-start | bytes 28
  7.7 19.6 %copy-start.3 = (f32[2]{0:T(128)S(1)}, f32[2]{0:T(128)}, u32[]{:S(2)}) copy-start(f32[2]{0:T(128)} %constant.120.clone) | copy-start | bytes 28
  7.7 23.6 %copy-start.5 = (s32[16]{0:T(128)S(1)}, s32[16]{0:T(128)}, u32[]{:S(2)}) copy-start(s32[16]{0:T(128)} %param.12) | copy-start | bytes 196
  7.7 42.3 %all-to-all-start = ((bf16[32,8,16,128]{3,2,1,0:T(8,128)(2,1)}), bf16[32,8,16,128]{3,2,1,0:T(8,128)(2,1)S(1)}, u32[]{:S(2)}, u32[]{:S(2)}) async-start(bf16[32,8,16,128]{3,2,1,0:T(8,128)(2,1)} %forward.1), calls=%async_computation | async-start | bytes 2097152 | tf_op jit(solution)/shard_map/all_to_all | solution.py:398
  25.9 1.3 %copy-start = (bf16[256,4096]{1,0:T(8,128)(2,1)}, bf16[256,4096]{1,0:T(8,128)(2,1)S(1)}, u32[]{:S(2)}) copy-start(bf16[256,4096]{1,0:T(8,128)(2,1)S(1)} %get-tuple-element.21.analysis_ref) | copy-start | bytes 6291460
  27.4 4.7 %collective-permute-start.1 = (f32[2,2,2048]{2,1,0:T(2,128)S(1)}, f32[2,2,2048]{2,1,0:T(2,128)S(1)}, u32[]{:S(2)}, u32[]{:S(2)}) collective-permute-start(f32[2,2,2048]{2,1,0:T(2,128)S(1)} %multiply_multiply_fusion), channel_id=1, source_target_pairs={{0,64},{32,96},{64,0},{96,32},{128,192},{160,224},{192,128},{224,1... | collective-permute-start | bytes 98312 | tf_op jit(solution)/shard_map/ppermute | solution.py:387
  30.2 3.1 %collective-permute-start = (f32[2,2,2048]{2,1,0:T(2,128)S(1)}, f32[2,2,2048]{2,1,0:T(2,128)S(1)}, u32[]{:S(2)}, u32[]{:S(2)}) collective-permute-start(f32[2,2,2048]{2,1,0:T(2,128)S(1)} %multiply_multiply_fusion), channel_id=1, source_target_pairs={{0,32},{32,0},{64,96},{96,64},{128,160},{160,128},{192,224},{224,1... | collective-permute-start | bytes 98312 | tf_op jit(solution)/shard_map/ppermute | solution.py:387
  30.5 4.3 %collective-permute-start.2 = (f32[2,2,2048]{2,1,0:T(2,128)S(1)}, f32[2,2,2048]{2,1,0:T(2,128)S(1)}, u32[]{:S(2)}, u32[]{:S(2)}) collective-permute-start(f32[2,2,2048]{2,1,0:T(2,128)S(1)} %multiply_multiply_fusion), channel_id=1, source_target_pairs={{0,96},{32,64},{64,32},{96,0},{128,224},{160,192},{192,160},{224,1... | collective-permute-start | bytes 98312 | tf_op jit(solution)/shard_map/ppermute | solution.py:387
  34.9 25.4 %collective-permute-start.3 = (f32[4,2,2,2048]{3,2,1,0:T(2,128)S(1)}, f32[4,2,2,2048]{3,2,1,0:T(2,128)S(1)}, u32[]{:S(2)}, u32[]{:S(2)}) collective-permute-start(f32[4,2,2,2048]{3,2,1,0:T(2,128)S(1)} %pad_maximum_fusion.near_ref), channel_id=1, source_target_pairs={{0,128},{32,160},{64,192},{96,224},{128,0},{160,32},{192,64},{224,... | collective-permute-start | bytes 393224 | tf_op jit(solution)/shard_map/ppermute | solution.py:387
  60.3 40.1 %all-to-all-start.1 = ((bf16[256,16,128]{2,1,0:T(8,128)(2,1)}), bf16[256,16,128]{2,1,0:T(8,128)(2,1)S(1)}, u32[]{:S(2)}, u32[]{:S(2)}) async-start(bf16[256,16,128]{2,1,0:T(8,128)(2,1)} %bitcast.6), calls=%async_computation.1 | async-start | bytes 2097152 | tf_op jit(solution)/shard_map/all_to_all | solution.py:409
